TPU v7x, 32 devices: a whole 2x2x4 slice. The times are simulated.
32 devices in a mesh: seq: 8 (over z, x), tp: 4 (over y, core).
Axes of the slice: x: 2, y: 2, z: 4, core: 2. Of those that a mesh axis runs over, the one named last changes fastest.
Arguments:
- inputs: bfloat16 [12288, 768], P(('seq', 'tp')), may hold values from -6 to 6
- lengths: int32 [169], replicated, may hold values from 20 to 128, as said below
- w_qkv: bfloat16 [3, 768, 768], P(None, None, 'tp'), may hold values from -0.21875 to 0.21875
- w_out: bfloat16 [768, 768], P('tp'), may hold values from -0.625 to 0.625
- w_in: bfloat16 [768, 2, 3072], P(None, None, 'tp'), may hold values from -0.21875 to 0.21875
- w_down: bfloat16 [3072, 768], P('tp'), may hold values from -0.109375 to 0.109375
- ln1_gain: float32 [768], replicated, may hold values from 0.5 to 1.5
- ln1_bias: float32 [768], replicated, may hold values from -1.2 to 1.2
- ln2_gain: float32 [768], replicated, may hold values from 0.5 to 1.5
- ln2_bias: float32 [768], replicated, may hold values from -1.2 to 1.2
- cotangent: bfloat16 [12288, 768], P(('seq', 'tp')), may hold values from -6 to 6
Outputs:
- layer_out: bfloat16 [12288, 768], P(('seq', 'tp'))
- grad_input: float32 [12288, 768], P(('seq', 'tp'))
- grad_w_qkv: float32 [3, 768, 768], P(None, None, 'tp')
- grad_w_out: float32 [768, 768], P('tp')
- grad_w_in: float32 [768, 2, 3072], P(None, None, 'tp')
- grad_w_down: float32 [3072, 768], P('tp')
- grad_ln1_gain: float32 [768], replicated
- grad_ln1_bias: float32 [768], replicated
- grad_ln2_gain: float32 [768], replicated
- grad_ln2_bias: float32 [768], replicated
Inputs may be any that keep to these rules, and one draw needn't show every extreme that they name: The 169 lengths add up to 12288. Every multiple of 1536 strictly between 0 and 12288 falls strictly inside a sequence, which has at most 127 tokens on either side of it.
All inputs are finite; a program needn't handle non-finite values.
Results may differ from a plain program's by a relative error of at most 0.02.
Values may be sent and summed in bfloat16 or wider, within the bound.
No kernel may reach another device: no remote copies, remote signals or barrier semaphores. Data moves between devices by JAX's collectives and lax.ppermute only.
A program may use at most 192 MiB of HBM per device.

v0:
```python
import math

import jax
import jax.numpy as jnp
import numpy as np
from jax import lax
from jax.sharding import PartitionSpec as P

HEADS = 12
HD = 64
LMAX = 128
REACH = 127
QBLOCK = 512


EPSILON = 1e-12
MASKED = -1e30


def with_halo(block, sides, width):
    for axis, dim in sides:
        count = lax.axis_size(axis)
        forward = [(i, i + 1) for i in range(count - 1)]
        backward = [(target, source) for source, target in forward]
        low = lax.ppermute(
            lax.slice_in_dim(block, block.shape[dim] - width, None, axis=dim), axis, forward
        )
        high = lax.ppermute(lax.slice_in_dim(block, 0, width, axis=dim), axis, backward)
        block = jnp.concatenate([low, block, high], axis=dim)
    return block


def slope_table(count):
    power_two = 2 ** int(math.floor(math.log2(count)))
    leading = [2.0 ** (-8.0 * (head + 1) / power_two) for head in range(power_two)]
    trailing = [2.0 ** (-4.0 * (2 * other + 1) / power_two) for other in range(count - power_two)]
    return np.array(leading + trailing, np.float32)


def layer_norm(values, norm_gain, norm_bias):
    centred = values - jnp.mean(values, axis=-1, keepdims=True)
    spread = jnp.mean(centred * centred, axis=-1, keepdims=True)
    return centred * lax.rsqrt(spread + EPSILON) * norm_gain + norm_bias


def sequence_ids(lengths, first_token, count, all_tokens):
    places = first_token + jnp.arange(count, dtype=jnp.int32)
    bounds = jnp.cumsum(lengths)
    located = jnp.searchsorted(bounds, places, side="right")
    inside = (places >= 0) & (places < all_tokens)
    return (jnp.where(inside, located, -1), places)


def block_scores(query_block, key_block, ids_query, ids_key, places_query, places_key, slopes):
    products = jnp.einsum(
        "qhd,khd->hqk", query_block, key_block, preferred_element_type=jnp.float32
    ) * HD ** (-0.5)
    distance = jnp.abs(places_query[:, None] - places_key[None, :]).astype(jnp.float32)
    scores = products - slopes[:, None, None] * distance[None]
    return jnp.where((ids_query[:, None] == ids_key[None, :])[None], scores, MASKED)


def gated_unit(gate_pair):
    return jax.nn.gelu(gate_pair[:, 0], approximate=False) * gate_pair[:, 1]


def per_device(
    inputs, lengths, w_qkv, w_out, w_in, w_down, ln1_gain, ln1_bias, ln2_gain, ln2_bias, cotangent
):
    tp_count = lax.axis_size("tp")
    own_rows = inputs.shape[0]
    tokens_here = own_rows * tp_count
    all_tokens = tokens_here * lax.axis_size("seq")
    head_width = w_qkv.shape[2]
    heads_here = head_width // HD
    slopes = lax.dynamic_slice_in_dim(
        jnp.asarray(slope_table(HEADS), jnp.float32), lax.axis_index("tp") * heads_here, heads_here
    )
    first_token = lax.axis_index("seq") * tokens_here
    ids_query, places_query = sequence_ids(lengths, first_token, tokens_here, all_tokens)
    ids_key, places_key = sequence_ids(
        lengths, first_token - LMAX, tokens_here + 2 * LMAX, all_tokens
    )
    window = QBLOCK + 2 * LMAX
    blocks = tokens_here // QBLOCK
    margin = LMAX - REACH
    gathered = lax.all_gather(inputs, "tp", axis=0, tiled=True)
    queries = jnp.dot(gathered, w_qkv[0], preferred_element_type=jnp.float32).astype(jnp.bfloat16)
    key_value = jnp.einsum(
        "nd,cde->nce", gathered, w_qkv[1:], preferred_element_type=jnp.float32
    ).astype(jnp.bfloat16)
    key_value = key_value.reshape(tokens_here, 2 * head_width)
    rimmed = with_halo(key_value, (("seq", 0),), REACH)
    padded = jnp.pad(rimmed, ((margin, margin), (0, 0)))

    def block_parts(block_index):
        row_start = block_index * QBLOCK
        query_block = queries[row_start : row_start + QBLOCK].reshape(QBLOCK, heads_here, HD)
        key_block = padded[row_start : row_start + window, :head_width].reshape(
            window, heads_here, HD
        )
        value_block = padded[row_start : row_start + window, head_width:].reshape(
            window, heads_here, HD
        )
        scores = block_scores(
            query_block,
            key_block,
            ids_query[row_start : row_start + QBLOCK],
            ids_key[row_start : row_start + window],
            places_query[row_start : row_start + QBLOCK],
            places_key[row_start : row_start + window],
            slopes,
        )
        return (query_block, key_block, value_block, scores)

    context_parts = []
    log_totals = []
    for block_index in range(blocks):
        query_block, key_block, value_block, scores = block_parts(block_index)
        highest = jnp.max(scores, axis=-1, keepdims=True)
        shifted = jnp.exp(scores - highest)
        summed = jnp.sum(shifted, axis=-1, keepdims=True)
        weights = (shifted / summed).astype(jnp.bfloat16)
        mixed_rows = jnp.einsum(
            "hqk,khd->qhd", weights, value_block, preferred_element_type=jnp.float32
        )
        context_parts.append(mixed_rows.astype(jnp.bfloat16).reshape(QBLOCK, head_width))
        log_totals.append(highest + jnp.log(summed))
    context = jnp.concatenate(context_parts, axis=0)
    attended = lax.psum_scatter(
        jnp.dot(context, w_out, preferred_element_type=jnp.float32),
        "tp",
        scatter_dimension=0,
        tiled=True,
    )
    normed, norm_one_back = jax.vjp(
        layer_norm, inputs.astype(jnp.float32) + attended, ln1_gain, ln1_bias
    )
    hidden_rows = lax.all_gather(normed.astype(jnp.bfloat16), "tp", axis=0, tiled=True)
    gate_up = jnp.einsum("nd,dcf->ncf", hidden_rows, w_in, preferred_element_type=jnp.float32)
    activated, gated_back = jax.vjp(gated_unit, gate_up)
    activated = activated.astype(jnp.bfloat16)
    branch = lax.psum_scatter(
        jnp.dot(activated, w_down, preferred_element_type=jnp.float32).astype(jnp.bfloat16),
        "tp",
        scatter_dimension=0,
        tiled=True,
    ).astype(jnp.float32)
    result, norm_two_back = jax.vjp(layer_norm, normed + branch, ln2_gain, ln2_bias)
    d_pre_two, d_gain_two, d_bias_two = norm_two_back(cotangent.astype(jnp.float32))
    d_branch = lax.all_gather(d_pre_two.astype(jnp.bfloat16), "tp", axis=0, tiled=True)
    grad_down = jnp.einsum("nf,nd->fd", activated, d_branch, preferred_element_type=jnp.float32)
    d_active = jnp.einsum("nd,fd->nf", d_branch, w_down, preferred_element_type=jnp.float32)
    d_gate_up = gated_back(d_active)[0].astype(jnp.bfloat16)
    grad_in = jnp.einsum("nd,ncf->dcf", hidden_rows, d_gate_up, preferred_element_type=jnp.float32)
    d_normed = d_pre_two + lax.psum_scatter(
        jnp.einsum("ncf,dcf->nd", d_gate_up, w_in, preferred_element_type=jnp.float32).astype(
            jnp.bfloat16
        ),
        "tp",
        scatter_dimension=0,
        tiled=True,
    ).astype(jnp.float32)
    d_pre_one, d_gain_one, d_bias_one = norm_one_back(d_normed)
    d_attended = lax.all_gather(d_pre_one.astype(jnp.bfloat16), "tp", axis=0, tiled=True)
    grad_out = jnp.einsum("ne,nd->ed", context, d_attended, preferred_element_type=jnp.float32)
    d_context = jnp.einsum(
        "nd,ed->ne", d_attended, w_out, preferred_element_type=jnp.float32
    ).astype(jnp.bfloat16)
    d_window = jnp.zeros((tokens_here + 2 * LMAX, 2 * head_width), jnp.float32)
    d_query_parts = []
    for block_index in range(blocks):
        query_block, key_block, value_block, scores = block_parts(block_index)
        row_start = block_index * QBLOCK
        weights = jnp.exp(scores - log_totals[block_index])
        d_rows = d_context[row_start : row_start + QBLOCK].reshape(QBLOCK, heads_here, HD)
        d_weights = jnp.einsum(
            "qhd,khd->hqk", d_rows, value_block, preferred_element_type=jnp.float32
        )
        row_dot = jnp.sum(d_weights * weights, axis=-1, keepdims=True)
        d_scores = (weights * (d_weights - row_dot)).astype(jnp.bfloat16)
        d_query_rows = jnp.einsum(
            "hqk,khd->qhd", d_scores, key_block, preferred_element_type=jnp.float32
        )
        d_query_parts.append(d_query_rows.reshape(QBLOCK, head_width) * HD ** (-0.5))
        d_keys = jnp.einsum(
            "hqk,qhd->khd", d_scores, query_block, preferred_element_type=jnp.float32
        ).reshape(window, head_width) * HD ** (-0.5)
        d_values = jnp.einsum(
            "hqk,qhd->khd", weights.astype(jnp.bfloat16), d_rows, preferred_element_type=jnp.float32
        ).reshape(window, head_width)
        d_window = d_window.at[row_start : row_start + window].add(
            jnp.concatenate([d_keys, d_values], axis=1)
        )
    rim_rows = jnp.concatenate(
        [d_window[margin:LMAX], d_window[LMAX + tokens_here : LMAX + tokens_here + REACH]], axis=0
    )
    returned = with_halo(rim_rows.astype(jnp.bfloat16), (("seq", 0),), REACH).astype(rim_rows.dtype)
    d_key_value = d_window[LMAX : LMAX + tokens_here]
    d_key_value = (
        d_key_value.at[:REACH]
        .add(returned[:REACH])
        .at[tokens_here - REACH :]
        .add(returned[3 * REACH :])
    )
    d_query = jnp.concatenate(d_query_parts, axis=0).astype(jnp.bfloat16)
    d_key_value = d_key_value.astype(jnp.bfloat16).reshape(tokens_here, 2, head_width)
    grad_query = jnp.einsum("nd,ne->de", gathered, d_query, preferred_element_type=jnp.float32)
    grad_key_value = jnp.einsum(
        "nd,nce->cde", gathered, d_key_value, preferred_element_type=jnp.float32
    )
    grad_qkv = jnp.concatenate([grad_query[None], grad_key_value], axis=0)
    query_part = jnp.einsum("ne,de->nd", d_query, w_qkv[0], preferred_element_type=jnp.float32)
    pair_part = jnp.einsum(
        "nce,cde->nd", d_key_value, w_qkv[1:], preferred_element_type=jnp.float32
    )
    grad_input = d_pre_one + lax.psum_scatter(
        (query_part + pair_part).astype(jnp.bfloat16), "tp", scatter_dimension=0, tiled=True
    ).astype(jnp.float32)
    grad_qkv, grad_out, grad_in, grad_down = lax.psum(
        (grad_qkv, grad_out, grad_in, grad_down), "seq"
    )
    norm_grads = lax.psum((d_gain_one, d_bias_one, d_gain_two, d_bias_two), ("seq", "tp"))
    return (
        result.astype(jnp.bfloat16),
        grad_input,
        grad_qkv,
        grad_out,
        grad_in,
        grad_down,
        norm_grads[0],
        norm_grads[1],
        norm_grads[2],
        norm_grads[3],
    )


def solution(mesh):
    in_specs = (
        P(("seq", "tp"), None),
        P(),
        P(None, None, "tp"),
        P("tp", None),
        P(None, None, "tp"),
        P("tp", None),
        P(),
        P(),
        P(),
        P(),
        P(("seq", "tp"), None),
    )
    out_specs = (
        P(("seq", "tp"), None),
        P(("seq", "tp"), None),
        P(None, None, "tp"),
        P("tp", None),
        P(None, None, "tp"),
        P("tp", None),
        P(),
        P(),
        P(),
        P(),
    )
    return jax.shard_map(
        per_device, mesh=mesh, in_specs=in_specs, out_specs=out_specs, check_vma=False
    )
```

profile of v0, /device:TPU:0, one launch (start us, length us, event | category | flops | bytes accessed | tf_op | source)
XLA Modules:
  0.0 865.8 jit_solution(4856376533249975018)
XLA Ops:
  9.3 88.0 %while.54 = (s32[]{:T(128)}, u32[1792]{0:T(1024)S(1)}, u32[1792]{0:T(1024)S(1)}, s32[169]{0:T(256)S(1)}, s32[]{:T(128)}, /*index=5*/s32[]{:T(128)}, s32[]{:T(128)}, s32[]{}) while((s32[]{:T(128)}, u32[1792]{0:T(1024)S(1)}, u32[1792]{0:T(1024)S(1)}, s32[169]{0:T(256)S(1)}, s32[]{:T(128)}, /*index=5*/s32[]{:T(128)}, s32[]{:T(128)}, ...), condition=%wide.region_5.6_spmd.clone, body=%wide.region_4.5_spmd.clone.sunk | while | flops 36100 | bytes 126577 | solution.py:49
  9.3 10.9 %gather_fusion.1 = s32[1792]{0:T(1024)S(1)} fusion(s32[169]{0:T(256)S(1)} %get-tuple-element.450, u32[2048]{0:T(1024)S(1)} %pad_clamp_fusion.5), kind=kCustom, calls=%fused_computation.1.clone.clone.1 | custom fusion | bytes 21504 | tf_op jit(solution)/shard_map/jit(searchsorted)/jit(_searchsorted_scan_impl)/vmap(jit(_searchsorted_scan_impl))/while/body/eval_jaxpr/gather | solution.py:49
  20.3 10.9 %gather_fusion.1 = s32[1792]{0:T(1024)S(1)} fusion(s32[169]{0:T(256)S(1)} %get-tuple-element.450, u32[2048]{0:T(1024)S(1)} %pad_clamp_fusion.5), kind=kCustom, calls=%fused_computation.1.clone.clone.1 | custom fusion | bytes 21504 | tf_op jit(solution)/shard_map/jit(searchsorted)/jit(_searchsorted_scan_impl)/vmap(jit(_searchsorted_scan_impl))/while/body/eval_jaxpr/gather | solution.py:49
  31.4 10.9 %gather_fusion.1 = s32[1792]{0:T(1024)S(1)} fusion(s32[169]{0:T(256)S(1)} %get-tuple-element.450, u32[2048]{0:T(1024)S(1)} %pad_clamp_fusion.5), kind=kCustom, calls=%fused_computation.1.clone.clone.1 | custom fusion | bytes 21504 | tf_op jit(solution)/shard_map/jit(searchsorted)/jit(_searchsorted_scan_impl)/vmap(jit(_searchsorted_scan_impl))/while/body/eval_jaxpr/gather | solution.py:49
  42.4 10.9 %gather_fusion.1 = s32[1792]{0:T(1024)S(1)} fusion(s32[169]{0:T(256)S(1)} %get-tuple-element.450, u32[2048]{0:T(1024)S(1)} %pad_clamp_fusion.5), kind=kCustom, calls=%fused_computation.1.clone.clone.1 | custom fusion | bytes 21504 | tf_op jit(solution)/shard_map/jit(searchsorted)/jit(_searchsorted_scan_impl)/vmap(jit(_searchsorted_scan_impl))/while/body/eval_jaxpr/gather | solution.py:49
  53.4 10.9 %gather_fusion.1 = s32[1792]{0:T(1024)S(1)} fusion(s32[169]{0:T(256)S(1)} %get-tuple-element.450, u32[2048]{0:T(1024)S(1)} %pad_clamp_fusion.5), kind=kCustom, calls=%fused_computation.1.clone.clone.1 | custom fusion | bytes 21504 | tf_op jit(solution)/shard_map/jit(searchsorted)/jit(_searchsorted_scan_impl)/vmap(jit(_searchsorted_scan_impl))/while/body/eval_jaxpr/gather | solution.py:49
  64.4 10.9 %gather_fusion.1 = s32[1792]{0:T(1024)S(1)} fusion(s32[169]{0:T(256)S(1)} %get-tuple-element.450, u32[2048]{0:T(1024)S(1)} %pad_clamp_fusion.5), kind=kCustom, calls=%fused_computation.1.clone.clone.1 | custom fusion | bytes 21504 | tf_op jit(solution)/shard_map/jit(searchsorted)/jit(_searchsorted_scan_impl)/vmap(jit(_searchsorted_scan_impl))/while/body/eval_jaxpr/gather | solution.py:49
  75.4 10.9 %gather_fusion.1 = s32[1792]{0:T(1024)S(1)} fusion(s32[169]{0:T(256)S(1)} %get-tuple-element.450, u32[2048]{0:T(1024)S(1)} %pad_clamp_fusion.5), kind=kCustom, calls=%fused_computation.1.clone.clone.1 | custom fusion | bytes 21504 | tf_op jit(solution)/shard_map/jit(searchsorted)/jit(_searchsorted_scan_impl)/vmap(jit(_searchsorted_scan_impl))/while/body/eval_jaxpr/gather | solution.py:49
  86.4 10.9 %gather_fusion.1 = s32[1792]{0:T(1024)S(1)} fusion(s32[169]{0:T(256)S(1)} %get-tuple-element.450, u32[2048]{0:T(1024)S(1)} %pad_clamp_fusion.5), kind=kCustom, calls=%fused_computation.1.clone.clone.1 | custom fusion | bytes 21504 | tf_op jit(solution)/shard_map/jit(searchsorted)/jit(_searchsorted_scan_impl)/vmap(jit(_searchsorted_scan_impl))/while/body/eval_jaxpr/gather | solution.py:49
  97.4 76.2 %while.53 = (s32[]{:T(128)}, u32[1536]{0:T(1024)S(1)}, u32[1536]{0:T(1024)S(1)}, s32[169]{0:T(256)S(1)}, s32[]{:T(128)}, /*index=5*/s32[]{:T(128)}, s32[]{:T(128)}, s32[]{}) while((s32[]{:T(128)}, u32[1536]{0:T(1024)S(1)}, u32[1536]{0:T(1024)S(1)}, s32[169]{0:T(256)S(1)}, s32[]{:T(128)}, /*index=5*/s32[]{:T(128)}, s32[]{:T(128)}, ...), condition=%wide.region_3.4_spmd.clone, body=%wide.region_2.3_spmd.clone.sunk | while | flops 31236 | bytes 109681 | solution.py:49
  97.4 9.4 %gather_fusion = s32[1536]{0:T(1024)S(1)} fusion(s32[169]{0:T(256)S(1)} %get-tuple-element.474, u32[2048]{0:T(1024)S(1)} %pad_clamp_fusion.4), kind=kCustom, calls=%fused_computation.clone.clone.1 | custom fusion | bytes 18432 | tf_op jit(solution)/shard_map/jit(searchsorted)/jit(_searchsorted_scan_impl)/vmap(jit(_searchsorted_scan_impl))/while/body/eval_jaxpr/gather | solution.py:49
  107.0 9.4 %gather_fusion = s32[1536]{0:T(1024)S(1)} fusion(s32[169]{0:T(256)S(1)} %get-tuple-element.474, u32[2048]{0:T(1024)S(1)} %pad_clamp_fusion.4), kind=kCustom, calls=%fused_computation.clone.clone.1 | custom fusion | bytes 18432 | tf_op jit(solution)/shard_map/jit(searchsorted)/jit(_searchsorted_scan_impl)/vmap(jit(_searchsorted_scan_impl))/while/body/eval_jaxpr/gather | solution.py:49
  116.5 9.4 %gather_fusion = s32[1536]{0:T(1024)S(1)} fusion(s32[169]{0:T(256)S(1)} %get-tuple-element.474, u32[2048]{0:T(1024)S(1)} %pad_clamp_fusion.4), kind=kCustom, calls=%fused_computation.clone.clone.1 | custom fusion | bytes 18432 | tf_op jit(solution)/shard_map/jit(searchsorted)/jit(_searchsorted_scan_impl)/vmap(jit(_searchsorted_scan_impl))/while/body/eval_jaxpr/gather | solution.py:49
  126.0 9.4 %gather_fusion = s32[1536]{0:T(1024)S(1)} fusion(s32[169]{0:T(256)S(1)} %get-tuple-element.474, u32[2048]{0:T(1024)S(1)} %pad_clamp_fusion.4), kind=kCustom, calls=%fused_computation.clone.clone.1 | custom fusion | bytes 18432 | tf_op jit(solution)/shard_map/jit(searchsorted)/jit(_searchsorted_scan_impl)/vmap(jit(_searchsorted_scan_impl))/while/body/eval_jaxpr/gather | solution.py:49
  135.5 9.4 %gather_fusion = s32[1536]{0:T(1024)S(1)} fusion(s32[169]{0:T(256)S(1)} %get-tuple-element.474, u32[2048]{0:T(1024)S(1)} %pad_clamp_fusion.4), kind=kCustom, calls=%fused_computation.clone.clone.1 | custom fusion | bytes 18432 | tf_op jit(solution)/shard_map/jit(searchsorted)/jit(_searchsorted_scan_impl)/vmap(jit(_searchsorted_scan_impl))/while/body/eval_jaxpr/gather | solution.py:49
  145.1 9.4 %gather_fusion = s32[1536]{0:T(1024)S(1)} fusion(s32[169]{0:T(256)S(1)} %get-tuple-element.474, u32[2048]{0:T(1024)S(1)} %pad_clamp_fusion.4), kind=kCustom, calls=%fused_computation.clone.clone.1 | custom fusion | bytes 18432 | tf_op jit(solution)/shard_map/jit(searchsorted)/jit(_searchsorted_scan_impl)/vmap(jit(_searchsorted_scan_impl))/while/body/eval_jaxpr/gather | solution.py:49
  154.6 9.4 %gather_fusion = s32[1536]{0:T(1024)S(1)} fusion(s32[169]{0:T(256)S(1)} %get-tuple-element.474, u32[2048]{0:T(1024)S(1)} %pad_clamp_fusion.4), kind=kCustom, calls=%fused_computation.clone.clone.1 | custom fusion | bytes 18432 | tf_op jit(solution)/shard_map/jit(searchsorted)/jit(_searchsorted_scan_impl)/vmap(jit(_searchsorted_scan_impl))/while/body/eval_jaxpr/gather | solution.py:49
  164.1 9.4 %gather_fusion = s32[1536]{0:T(1024)S(1)} fusion(s32[169]{0:T(256)S(1)} %get-tuple-element.474, u32[2048]{0:T(1024)S(1)} %pad_clamp_fusion.4), kind=kCustom, calls=%fused_computation.clone.clone.1 | custom fusion | bytes 18432 | tf_op jit(solution)/shard_map/jit(searchsorted)/jit(_searchsorted_scan_impl)/vmap(jit(_searchsorted_scan_impl))/while/body/eval_jaxpr/gather | solution.py:49
  181.3 2.7 convolution_convert_fusion.2
  186.2 5.6 collective-permute-start
  193.2 1.7 fusion.97
  197.2 2.8 fusion.60
  200.0 3.1 concatenate.38
  203.1 2.0 pad_slice_fusion.2
  205.2 1.7 fusion.98
  209.0 1.6 fusion.61
  210.7 1.7 fusion.96
  214.6 1.6 fusion.59
  216.8 3.0 fusion.71
  220.0 50.3 %reduce-scatter.5.cloned.1.call-done = f32[384,768]{1,0:T(8,128)} async-done(((f32[1536,768]{1,0:T(8,128)}), f32[384,768]{1,0:T(8,128)}) %reduce-scatter.5.cloned.1.call-update) | async-done | bytes 1179664 | tf_op jit(solution)/shard_map/reduce_scatter | solution.py:130
  270.3 1.6 fusion.87
  274.1 24.0 %all-gather.7.cloned.1.call-done = bf16[1536,768]{1,0:T(8,128)(2,1)} async-done(((bf16[384,768]{1,0:T(8,128)(2,1)}), bf16[1536,768]{1,0:T(8,128)(2,1)}) %all-gather.7.cloned.1.call-update) | async-done | bytes 2359312 | tf_op jit(solution)/shard_map/all_gather | solution.py:139
  298.1 5.5 fusion.41
  303.7 11.5 %multiply_convert_fusion.3 = (bf16[1536,768]{1,0:T(8,128)(2,1)S(1)}, f32[1536,768]{1,0:T(8,128)}) fusion(f32[1536,2,768]{2,0,1:T(8,128)S(1)} %fusion.41), kind=kLoop, calls=%fused_computation.44 | loop fusion | flops 77856768 | bytes 16515072 | tf_op jit(solution)/shard_map/convert_element_type | solution.py:142
  316.5 3.4 convolution_convert_fusion
  320.1 33.2 %reduce-scatter.7.cloned.1.call-done = bf16[384,768]{1,0:T(8,128)(2,1)} async-done(((bf16[1536,768]{1,0:T(8,128)(2,1)}), bf16[384,768]{1,0:T(8,128)(2,1)}) %reduce-scatter.7.cloned.1.call-update) | async-done | bytes 589840 | tf_op jit(solution)/shard_map/reduce_scatter | solution.py:143
  353.2 1.6 fusion.85
  355.1 1.8 fusion.57
  356.9 2.1 fusion.84
  361.0 24.2 %all-gather.9.cloned.1.call-done = bf16[1536,768]{1,0:T(8,128)(2,1)} async-done(((bf16[384,768]{1,0:T(8,128)(2,1)}), bf16[1536,768]{1,0:T(8,128)(2,1)}) %all-gather.9.cloned.1.call-update) | async-done | bytes 2359312 | tf_op jit(solution)/shard_map/all_gather | solution.py:151
  385.2 9.6 %multiply_bitcast_fusion = (f32[1536,1,768]{2,0,1:T(8,128)S(1)}, f32[1536,1,768]{2,0,1:T(8,128)S(1)}) fusion(f32[1536,768]{1,0:T(8,128)} %get-tuple-element.311, f32[1536,2,768]{2,0,1:T(8,128)} %copy-done.11, bf16[1536,768]{1,0:T(8,128)(2,1)} %all-gather.9.cloned.1.call-done, bf16[768,768]{1,0:T(8,128)(2,1)} %param.31), kind=kOutput, calls=%fused_computation.43 | convolution fusion | flops 1830813696 | bytes 27131904 | tf_op jit(solution)/shard_map/nd,fd->nf/dot_general | solution.py:153
  394.8 2.1 copy-done.83
  397.0 1.6 copy-done.84
  398.5 5.1 bitcast_convert_fusion
  403.7 33.2 %reduce-scatter.9.cloned.1.call-done = bf16[384,768]{1,0:T(8,128)(2,1)} async-done(((bf16[1536,768]{1,0:T(8,128)(2,1)}), bf16[384,768]{1,0:T(8,128)(2,1)}) %reduce-scatter.9.cloned.1.call-update) | async-done | bytes 589840 | tf_op jit(solution)/shard_map/reduce_scatter | solution.py:156
  436.9 2.4 multiply_reduce_fusion.3
  441.4 23.8 %all-gather.11.cloned.1.call-done = bf16[1536,768]{1,0:T(8,128)(2,1)} async-done(((bf16[384,768]{1,0:T(8,128)(2,1)}), bf16[1536,768]{1,0:T(8,128)(2,1)}) %all-gather.11.cloned.1.call-update) | async-done | bytes 2359312 | tf_op jit(solution)/shard_map/all_gather | solution.py:165
  465.2 2.6 convolution_convert_fusion.1
  467.9 3.4 fusion.35
  471.3 3.8 multiply_reduce_fusion.2
  479.4 1.5 multiply_reduce_fusion
  482.0 1.5 fusion.64
  485.1 1.5 multiply_reduce_fusion.1
  490.5 5.0 collective-permute-start.2
  495.5 1.5 fusion.63
  501.2 2.6 fusion.80
  503.8 2.3 fusion.5
  506.2 1.6 copy-done.10
  507.8 5.3 fusion.100
  513.1 10.2 %fusion.39 = f32[768,2,768]{2,0,1:T(8,128)} fusion(bf16[1536,768]{1,0:T(8,128)(2,1)S(1)} %copy-done.79, f32[1536,1,768]{2,0,1:T(8,128)} %copy-done.84, f32[1536,1,768]{2,0,1:T(8,128)} %copy-done.83), kind=kOutput, calls=%fused_computation.84 | convolution fusion | flops 3628597248 | bytes 16515072 | tf_op jit(solution)/shard_map/nd,ncf->dcf/dot_general | solution.py:155
  530.2 43.6 %all-reduce.5 = (f32[768]{0:T(1024)}, f32[768]{0:T(1024)}, f32[768]{0:T(1024)}, f32[768]{0:T(1024)}) all-reduce(f32[768]{0:T(1024)S(1)} %copy-done.75, f32[768]{0:T(1024)S(1)} %copy-done.76, f32[768]{0:T(1024)S(1)} %copy-done.73, f32[768]{0:T(1024)S(1)} %copy-done.74), channel_id=1, replica_groups=mesh['seq'=8,'tp'=4] {'seq','tp'}, use_global_device_ids=true, to_apply=%region_32.33 | all-reduce | flops 3072 | bytes 24576 | tf_op jit(solution)/shard_map/psum | solution.py:223
  573.8 2.3 convert_add_fusion
  576.1 270.7 %all-reduce.9.cloned.1.call-done = (f32[3,768,192]{1,2,0:T(8,128)}, f32[192,768]{1,0:T(8,128)}, f32[768,2,768]{2,0,1:T(8,128)}, f32[768,768]{1,0:T(8,128)}) async-done(((f32[3,768,192]{1,2,0:T(8,128)}, f32[192,768]{1,0:T(8,128)}, f32[768,2,768]{2,0,1:T(8,128)}, f32[768,768]{1,0:T(8,128)}), (f32[3,768,192]{1,2,0:T(8,128)}, f32[192,768]{1,0:T(8,128)}, f32[768,2,768]{2,0,1:T(8,128)}, ...) | async-done | bytes 9437200 | tf_op jit(solution)/shard_map/psum | solution.py:220
  846.8 8.3 copy.29
  (366 shorter events, 54.8 us)
Async XLA Ops:
  7.2 290.9 %copy-start = (bf16[768,2,768]{2,1,0:T(2,128)(2,1)S(1)}, bf16[768,2,768]{2,1,0:T(2,128)(2,1)}, u32[]{:S(2)}) copy-start(bf16[768,2,768]{2,1,0:T(2,128)(2,1)} %param.30) | copy-start | bytes 7077892
  7.2 174.1 %all-gather.5.cloned.1.call-start = ((), (), s32[]{:S(2)}) async-start(), calls=%async_computation.4 | async-start | bytes 2949120 | tf_op jit(solution)/shard_map/all_gather | solution.py:87
  7.9 262.4 %reduce-scatter.5.cloned.1.call-start = ((), (), s32[]{:S(2)}) async-start(), calls=%async_computation.5 | async-start | bytes 5898240 | tf_op jit(solution)/shard_map/reduce_scatter | solution.py:130
  97.4 76.2 %copy-start.82 = (f32[12]{0:T(128)S(1)}, f32[12]{0:T(128)}, u32[]{:S(2)}) copy-start(f32[12]{0:T(128)} %constant.312.clone) | copy-start | bytes 148
  176.9 4.4 copy-start.31
  181.3 3.6 slice-start.6
  181.3 3.6 copy-start.77
  184.8 8.4 copy-start.33
  185.9 7.3 copy-start.18
  185.9 7.2 copy-start.48
  186.2 13.8 %collective-permute-start = (bf16[127,384]{0,1:T(8,128)(2,1)S(1)}, bf16[127,384]{0,1:T(8,128)(2,1)}, u32[]{:S(2)}, u32[]{:S(2)}) collective-permute-start(bf16[127,384]{0,1:T(8,128)(2,1)S(1)} %bitcast.276), channel_id=1, source_target_pairs={{0,4},{4,8},{8,12},{12,16},{16,20},{20,24},{24,28},{1,5},{5,9},{9,... | collective-permute-start | bytes 292616 | tf_op jit(solution)/shard_map/ppermute | solution.py:25
  191.8 8.2 collective-permute-start.1
  193.2 3.2 copy-start.23
  194.9 2.2 copy-start.2
  196.4 3.6 copy-start.60
  205.1 3.2 copy-start.21
  205.1 5.5 copy-start.25
  205.1 8.7 %copy-start.19 = (bf16[768,192]{0,1:T(8,128)(2,1)}, bf16[768,192]{0,1:T(8,128)(2,1)S(1)}, u32[]{:S(2)}) copy-start(bf16[768,192]{0,1:T(8,128)(2,1)S(1)} %get-tuple-element.317) | copy-start | bytes 884740
  208.3 2.3 copy-start.64
  210.6 5.5 copy-start.53
  213.8 2.3 copy-start.68
  214.6 2.3 copy-start.49
  214.6 2.3 copy-start.51
  219.9 52.9 %copy-start.57 = (f32[768]{0:T(1024)S(1)}, f32[768]{0:T(1024)}, u32[]{:S(2)}) copy-start(f32[768]{0:T(1024)} %param.32) | copy-start | bytes 9220
  219.9 52.9 %copy-start.72 = (f32[768]{0:T(1024)S(1)}, f32[768]{0:T(1024)}, u32[]{:S(2)}) copy-start(f32[768]{0:T(1024)} %param.33) | copy-start | bytes 9220
  219.9 78.2 %all-gather.7.cloned.1.call-start = ((), (), s32[]{:S(2)}) async-start(), calls=%async_computation.6 | async-start | bytes 2949120 | tf_op jit(solution)/shard_map/all_gather | solution.py:139
  273.9 79.4 %reduce-scatter.7.cloned.1.call-start = ((), (), s32[]{:S(2)}) async-start(), calls=%async_computation.7 | async-start | bytes 2949120 | tf_op jit(solution)/shard_map/reduce_scatter | solution.py:143
  303.6 11.5 %copy-start.11 = (f32[1536,2,768]{2,0,1:T(8,128)}, f32[1536,2,768]{2,0,1:T(8,128)S(1)}, u32[]{:S(2)}) copy-start(f32[1536,2,768]{2,0,1:T(8,128)S(1)} %fusion.41) | copy-start | bytes 28311556
  303.6 12.9 %copy-start.81 = (bf16[768,768]{1,0:T(8,128)(2,1)S(1)}, bf16[768,768]{1,0:T(8,128)(2,1)}, u32[]{:S(2)}) copy-start(bf16[768,768]{1,0:T(8,128)(2,1)} %param.31) | copy-start | bytes 3538948
  320.0 65.2 %all-gather.9.cloned.1.call-start = ((), (), s32[]{:S(2)}) async-start(), calls=%async_computation.8 | async-start | bytes 2949120 | tf_op jit(solution)/shard_map/all_gather | solution.py:151
  361.0 75.9 %reduce-scatter.9.cloned.1.call-start = ((), (), s32[]{:S(2)}) async-start(), calls=%async_computation.9 | async-start | bytes 2949120 | tf_op jit(solution)/shard_map/reduce_scatter | solution.py:156
  394.8 3.7 copy-start.84
  403.6 33.3 %copy-start.6 = (f32[384,768]{1,0:T(8,128)S(1)}, f32[384,768]{1,0:T(8,128)}, u32[]{:S(2)}) copy-start(f32[384,768]{1,0:T(8,128)} %copy-done.5) | copy-start | bytes 3538948
  403.6 35.6 %copy-start.71 = (f32[384]{0:T(512)S(1)}, f32[384]{0:T(512)}, u32[]{:S(2)}) copy-start(f32[384]{0:T(512)} %copy-done.70) | copy-start | bytes 4612
  403.7 61.6 %all-gather.11.cloned.1.call-start = ((), (), s32[]{:S(2)}) async-start(), calls=%async_computation.10 | async-start | bytes 2949120 | tf_op jit(solution)/shard_map/all_gather | solution.py:165
  436.9 2.4 copy-start.12
  439.9 27.9 %copy-start.7 = (f32[384,768]{1,0:T(8,128)}, f32[384,768]{1,0:T(8,128)S(1)}, u32[]{:S(2)}) copy-start(f32[384,768]{1,0:T(8,128)S(1)} %get-tuple-element.305) | copy-start | bytes 3538948
  440.0 25.2 %copy-start.50 = (bf16[192,768]{1,0:T(8,128)(2,1)S(1)}, bf16[192,768]{1,0:T(8,128)(2,1)}, u32[]{:S(2)}) copy-start(bf16[192,768]{1,0:T(8,128)(2,1)} %param.29) | copy-start | bytes 884740
  441.0 132.8 %reduce-scatter.11.cloned.1.call-start = ((), (), s32[]{:S(2)}) async-start(), calls=%async_computation.11 | async-start | bytes 2949120 | tf_op jit(solution)/shard_map/reduce_scatter | solution.py:217
  467.9 3.5 copy-start.22
  467.9 7.3 slice-start.4
  471.3 3.9 slice-start.5
  475.2 3.2 slice-start.2
  475.2 3.2 slice-start.3
  480.9 3.2 slice-start
  480.9 3.2 slice-start.1
  488.7 6.8 copy-start.30
  489.2 8.1 collective-permute-start.3
  490.5 7.5 collective-permute-start.2
  501.2 2.7 copy-start.32
  501.2 2.6 copy-start.39
  501.2 2.6 copy-start.41
  501.2 2.6 copy-start.43
  506.1 340.6 %all-reduce.9.cloned.1.call-start = ((), (), s32[]{:S(2)}) async-start(), calls=%async_computation.12 | async-start | bytes 18874368 | tf_op jit(solution)/shard_map/psum | solution.py:220
  507.8 5.3 copy-start.79
  513.0 10.2 %copy-start.40 = (bf16[3,64,512]{2,1,0:T(8,128)(2,1)S(1)}, bf16[3,64,512]{2,1,0:T(8,128)(2,1)}, u32[]{:S(2)}) copy-start(bf16[3,64,512]{2,1,0:T(8,128)(2,1)} %fusion.62) | copy-start | bytes 589828
  513.0 10.2 %copy-start.42 = (bf16[3,64,512]{2,1,0:T(8,128)(2,1)S(1)}, bf16[3,64,512]{2,1,0:T(8,128)(2,1)}, u32[]{:S(2)}) copy-start(bf16[3,64,512]{2,1,0:T(8,128)(2,1)} %fusion.64) | copy-start | bytes 589828
  513.1 10.2 %copy-start.44 = (bf16[3,64,512]{2,1,0:T(8,128)(2,1)S(1)}, bf16[3,64,512]{2,1,0:T(8,128)(2,1)}, u32[]{:S(2)}) copy-start(bf16[3,64,512]{2,1,0:T(8,128)(2,1)} %fusion.63) | copy-start | bytes 589828
  513.1 10.2 %copy-start.78 = (bf16[1536,768]{1,0:T(8,128)(2,1)S(1)}, bf16[1536,768]{1,0:T(8,128)(2,1)}, u32[]{:S(2)}) copy-start(bf16[1536,768]{1,0:T(8,128)(2,1)} %all-gather.5.cloned.1.call-done) | copy-start | bytes 7077892
  523.3 2.3 copy-start.80
  529.5 44.3 %copy-start.8 = (f32[384,768]{1,0:T(8,128)S(1)}, f32[384,768]{1,0:T(8,128)}, u32[]{:S(2)}) copy-start(f32[384,768]{1,0:T(8,128)} %copy-done.7) | copy-start | bytes 3538948
  846.7 8.3 copy-start.15
  855.0 2.7 copy-start.13
  856.5 2.6 copy-start.1
  (41 other events, 58.4 us)
Sparse Core Ops, SparseCore 0:
  9.6 26.7 all-gather.4
  220.0 50.2 reduce-scatter.4
  274.0 24.0 all-gather.6
  320.1 33.0 reduce-scatter.6
  361.1 24.0 all-gather.8
  403.8 33.0 reduce-scatter.8
  441.1 24.0 all-gather.10
  506.2 34.3 reduce-scatter.10
  545.7 301.0 all-reduce.8
where the time goes:
time: 872 us; the launch traced here: 866 us
  waiting for transfers between devices  461 us (53%)
  local copies, waits for them, and re-layouts  199 us (23%)
  matrix products  86 us (10%)
  other arithmetic  46 us (5%)
  blocking collectives  43.6 us (5%)
  between operations  15.3 us (2%)
  starting transfers between devices  13.9 us (2%)
    psum x1, waiting for transfers between devices, per_device(): lax.psum((grad_qkv, grad_out, grad_in, grad_down), 'seq')  271 us
    gather x16, local copies, waits for them, and re-layouts, sequence_ids(): located = jnp.searchsorted(bounds, places, side='right')  163 us
    reduce_scatter x1, waiting for transfers between devices, per_device(): lax.psum_scatter(jnp.dot(context, w_out, preferred_element_type=jnp.float...  50.3 us
    psum x1, blocking collectives, per_device(): lax.psum((d_gain_one, d_bias_one, d_gain_two, d_bias_two), ('seq', 'tp'))  43.6 us
    reduce_scatter x1, waiting for transfers between devices, per_device(): lax.psum_scatter(jnp.einsum('ncf,dcf->nd', d_gate_up, w_in, preferred_ele...  33.2 us
    reduce_scatter x1, waiting for transfers between devices, per_device(): lax.psum_scatter(jnp.dot(activated, w_down, preferred_element_type=jnp.fl...  33.2 us
    unnamed x186, local copies, waits for them, and re-layouts  26.2 us
    all_gather x1, waiting for transfers between devices, per_device(): lax.all_gather(d_pre_two.astype(jnp.bfloat16), 'tp', axis=0, tiled=True)  24.2 us
  transfers between devices with their start and end apart: 13, of which 8 were waited for; matrix products, arithmetic and copies ran while one was open for 23% of the time, Pallas kernels for 0%

commit v1 on v0

v1 whole, which is shorter than its diff:
```python
import functools
import math

import jax
import jax.numpy as jnp
import numpy as np
from jax import lax
from jax.experimental import pallas as pl
from jax.experimental.pallas import tpu as pltpu
from jax.sharding import PartitionSpec as P

HEADS = 12
HD = 64
QB = 128
WINDOW = 3 * QB
EPSILON = 1e-12
FAR = 1e30

BF = jnp.bfloat16
F32 = jnp.float32
VMEM_LIMIT = 40 * 1024 * 1024


def dot(a, b, ca, cb):
    return lax.dot_general(a, b, (((ca,), (cb,)), ((), ())), preferred_element_type=F32)


def slope_table(count):
    power_two = 2 ** int(math.floor(math.log2(count)))
    leading = [2.0 ** (-8.0 * (head + 1) / power_two) for head in range(power_two)]
    trailing = [2.0 ** (-4.0 * (2 * other + 1) / power_two) for other in range(count - power_two)]
    return np.array(leading + trailing, np.float32)


def smem():
    return pl.BlockSpec(memory_space=pltpu.SMEM)


def full(shape):
    return pl.BlockSpec(shape, lambda *_: (0,) * len(shape))


def cost(flops, moved, transcendentals=0):
    return pl.CostEstimate(flops=flops, bytes_accessed=moved, transcendentals=transcendentals)


def params():
    return pltpu.CompilerParams(vmem_limit_bytes=VMEM_LIMIT)


def block_distance(se_ref, off):
    start = se_ref[0:1, pl.ds(off, QB)] - off
    end = se_ref[1:2, pl.ds(off, QB)] - off
    key = lax.broadcasted_iota(jnp.int32, (WINDOW, QB), 0)
    query = lax.broadcasted_iota(jnp.int32, (WINDOW, QB), 1) + QB
    valid = (key >= start) & (key < end)
    return jnp.where(valid, jnp.abs(key - query).astype(F32), FAR)


def block_probs(key, query, slope, distance):
    scores = dot(key, query, 1, 0) - slope * distance
    shifted = jnp.exp(scores - jnp.max(scores, axis=0, keepdims=True))
    return shifted * (1.0 / jnp.sum(shifted, axis=0, keepdims=True))


def attn_fwd_kernel(heads, slopes_ref, se_ref, qkv_ref, kv_ref, ctx_ref):
    width = heads * HD

    def block(b, carry):
        off = pl.multiple_of(b * QB, QB)
        distance = block_distance(se_ref, off)
        for h in range(heads):
            rows = slice(h * HD, (h + 1) * HD)
            query = qkv_ref[rows, pl.ds(off + QB, QB)] * BF(0.125)
            key = kv_ref[pl.ds(off, WINDOW), h * 128 : h * 128 + HD]
            probs = block_probs(key, query, slopes_ref[h], distance).astype(BF)
            value = qkv_ref[2 * width + h * HD : 2 * width + (h + 1) * HD, pl.ds(off, WINDOW)]
            ctx_ref[rows, pl.ds(off, QB)] = dot(value, probs, 1, 0).astype(BF)
        return carry

    lax.fori_loop(0, ctx_ref.shape[1] // QB, block, 0)


def attn_fwd(heads, slopes, se, qkv, kv):
    rows = se.shape[1]
    elements = heads * rows * WINDOW
    return pl.pallas_call(
        functools.partial(attn_fwd_kernel, heads),
        out_shape=jax.ShapeDtypeStruct((heads * HD, rows), BF),
        in_specs=[smem()] + [pl.BlockSpec(memory_space=pltpu.VMEM)] * 3,
        out_specs=pl.BlockSpec(memory_space=pltpu.VMEM),
        compiler_params=params(),
        cost_estimate=cost(elements * HD * 16, qkv.size * 2 + kv.size * 2, elements),
        name="attention_forward",
    )(slopes, se, qkv, kv)


def attn_bwd_kernel(heads, slopes_ref, se_ref, qkv_ref, kv_ref, dctx_ref, out_ref, acc_ref):
    width = heads * HD
    rows = dctx_ref.shape[1]
    acc_ref[...] = jnp.zeros_like(acc_ref)
    out_ref[0:width, 0:QB] = jnp.zeros((width, QB), BF)
    out_ref[0:width, QB + rows :] = jnp.zeros((width, QB), BF)

    def block(b, carry):
        off = pl.multiple_of(b * QB, QB)
        distance = block_distance(se_ref, off)
        for h in range(heads):
            mine = slice(h * HD, (h + 1) * HD)
            query = qkv_ref[mine, pl.ds(off + QB, QB)] * BF(0.125)
            key = kv_ref[pl.ds(off, WINDOW), h * 128 : h * 128 + HD]
            value = kv_ref[pl.ds(off, WINDOW), (heads + h) * 128 : (heads + h) * 128 + HD]
            probs = block_probs(key, query, slopes_ref[h], distance)
            d_rows = dctx_ref[mine, pl.ds(off, QB)]
            d_probs = dot(value, d_rows, 1, 0)
            row_dot = jnp.sum(d_probs * probs, axis=0, keepdims=True)
            d_scores = (probs * (d_probs - row_dot)).astype(BF)
            key_t = qkv_ref[width + h * HD : width + (h + 1) * HD, pl.ds(off, WINDOW)]
            d_query = dot(key_t, d_scores, 1, 0) * 0.125
            out_ref[mine, pl.ds(off + QB, QB)] = d_query.astype(BF)
            acc_ref[mine, pl.ds(off, WINDOW)] += dot(query, d_scores, 1, 1)
            acc_ref[width + h * HD : width + (h + 1) * HD, pl.ds(off, WINDOW)] += dot(
                d_rows, probs.astype(BF), 1, 1
            )
        return carry

    lax.fori_loop(0, rows // QB, block, 0)
    out_ref[width:, :] = acc_ref[...].astype(BF)


def attn_bwd(heads, slopes, se, qkv, kv, dctx):
    rows = se.shape[1]
    elements = heads * rows * WINDOW
    return pl.pallas_call(
        functools.partial(attn_bwd_kernel, heads),
        out_shape=jax.ShapeDtypeStruct(qkv.shape, BF),
        in_specs=[smem()] + [pl.BlockSpec(memory_space=pltpu.VMEM)] * 4,
        out_specs=pl.BlockSpec(memory_space=pltpu.VMEM),
        scratch_shapes=[pltpu.VMEM((2 * heads * HD, qkv.shape[1]), F32)],
        compiler_params=params(),
        cost_estimate=cost(elements * HD * 40, qkv.size * 4 + kv.size * 2, elements),
        name="attention_backward",
    )(slopes, se, qkv, kv, dctx)


def phi_pair(gate):
    bell = jnp.exp(gate * gate * -0.5)
    t = 1.0 / (1.0 + (0.3275911 / math.sqrt(2.0)) * jnp.abs(gate))
    poly = t * (
        0.254829592
        + t * (-0.284496736 + t * (1.421413741 + t * (-1.453152027 + t * 1.061405429)))
    )
    tail = 0.5 * poly * bell
    return jnp.where(gate >= 0.0, 1.0 - tail, tail), bell * (1.0 / math.sqrt(2.0 * math.pi))


def ff_fwd_kernel(x_ref, wg_ref, wu_ref, wd_ref, act_ref, a_ref, b_ref, keep_ref, send_ref):
    x = x_ref[...]
    hidden = wd_ref.shape[0]
    for f in range(0, hidden, 256):
        cols = slice(f, f + 256)
        gate = dot(x, wg_ref[:, cols], 1, 0)
        up = dot(x, wu_ref[:, cols], 1, 0)
        big, small = phi_pair(gate)
        gelu = gate * big
        act_ref[:, cols] = (gelu * up).astype(BF)
        a_ref[:, cols] = gelu.astype(BF)
        b_ref[:, cols] = (up * (big + gate * small)).astype(BF)
    part = dot(act_ref[...], wd_ref[...], 1, 0).astype(BF)

    @pl.when(pl.program_id(0) == 0)
    def _():
        keep_ref[...] = part

    @pl.when(pl.program_id(0) == 1)
    def _():
        send_ref[...] = part


def ff_fwd(x, wg, wu, wd):
    rows, width = x.shape
    hidden = wd.shape[0]
    half = rows // 2
    tile = pl.BlockSpec((half, hidden), lambda i: (i, 0))
    return pl.pallas_call(
        ff_fwd_kernel,
        grid=(2,),
        out_shape=[jax.ShapeDtypeStruct((rows, hidden), BF)] * 3
        + [jax.ShapeDtypeStruct((half, width), BF)] * 2,
        in_specs=[pl.BlockSpec((half, width), lambda i: (i, 0))]
        + [full((width, hidden))] * 2
        + [full((hidden, width))],
        out_specs=[tile] * 3 + [full((half, width))] * 2,
        compiler_params=params(),
        cost_estimate=cost(rows * width * hidden * 6, 12 * rows * width, 2 * rows * hidden),
        name="ff_forward",
    )(x, wg, wu, wd)


def ff_bwd_kernel(
    db_ref, a_ref, b_ref, wdt_ref, wgt_ref, wut_ref, dg_ref, du_ref, keep_ref, send_ref
):
    db = db_ref[...]
    hidden = wdt_ref.shape[1]
    for f in range(0, hidden, 256):
        cols = slice(f, f + 256)
        d_active = dot(db, wdt_ref[:, cols], 1, 0)
        dg_ref[:, cols] = (d_active * b_ref[:, cols].astype(F32)).astype(BF)
        du_ref[:, cols] = (d_active * a_ref[:, cols].astype(F32)).astype(BF)
    part = (dot(dg_ref[...], wgt_ref[...], 1, 0) + dot(du_ref[...], wut_ref[...], 1, 0)).astype(BF)

    @pl.when(pl.program_id(0) == 0)
    def _():
        keep_ref[...] = part

    @pl.when(pl.program_id(0) == 1)
    def _():
        send_ref[...] = part


def ff_bwd(db, a, b, wdt, wgt, wut):
    rows, width = db.shape
    hidden = wdt.shape[1]
    half = rows // 2
    tile = pl.BlockSpec((half, hidden), lambda i: (i, 0))
    return pl.pallas_call(
        ff_bwd_kernel,
        grid=(2,),
        out_shape=[jax.ShapeDtypeStruct((rows, hidden), BF)] * 2
        + [jax.ShapeDtypeStruct((half, width), BF)] * 2,
        in_specs=[pl.BlockSpec((half, width), lambda i: (i, 0)), tile, tile]
        + [full((width, hidden))]
        + [full((hidden, width))] * 2,
        out_specs=[tile] * 2 + [full((half, width))] * 2,
        compiler_params=params(),
        cost_estimate=cost(rows * width * hidden * 6, 12 * rows * width),
        name="ff_backward",
    )(db, a, b, wdt, wgt, wut)


def centre(pre):
    mean = jnp.mean(pre, axis=-1, keepdims=True)
    centred = pre - mean
    r = lax.rsqrt(jnp.mean(centred * centred, axis=-1, keepdims=True) + EPSILON)
    return centred * r, r


def norm_back(xhat, r, gain, grad):
    e = grad * gain
    return r * (
        e
        - jnp.mean(e, axis=-1, keepdims=True)
        - xhat * jnp.mean(e * xhat, axis=-1, keepdims=True)
    )


def ln1_kernel(x_ref, own_ref, recv_ref, gain_ref, bias_ref, pre_ref, normed_ref, low_ref):
    pre = x_ref[...].astype(F32) + (own_ref[...] + recv_ref[...].astype(F32))
    pre_ref[...] = pre
    xhat, _ = centre(pre)
    normed = xhat * gain_ref[...] + bias_ref[...]
    normed_ref[...] = normed
    low_ref[...] = normed.astype(BF)


def ln1(x, own, recv, gain, bias):
    shape = x.shape
    vm = pl.BlockSpec(memory_space=pltpu.VMEM)
    return pl.pallas_call(
        ln1_kernel,
        out_shape=[
            jax.ShapeDtypeStruct(shape, F32),
            jax.ShapeDtypeStruct(shape, F32),
            jax.ShapeDtypeStruct(shape, BF),
        ],
        in_specs=[vm] * 5,
        out_specs=[vm] * 3,
        compiler_params=params(),
        cost_estimate=cost(x.size * 10, x.size * 18),
        name="norm_one",
    )(x, own, recv, gain, bias)


def ln2_kernel(
    normed_ref, keep_ref, near_ref, far_ref, dy_ref, gain_ref, bias_ref,
    out_ref, d_ref, low_ref, grads_ref,
):
    branch = (
        keep_ref[...].astype(F32) + near_ref[...].astype(F32) + far_ref[...].astype(F32)
    )
    xhat, r = centre(normed_ref[...] + branch)
    gain = gain_ref[...]
    out_ref[...] = (xhat * gain + bias_ref[...]).astype(BF)
    dy = dy_ref[...].astype(F32)
    d = norm_back(xhat, r, gain, dy)
    d_ref[...] = d
    low_ref[...] = d.astype(BF)
    grads_ref[0:1, :] = jnp.sum(dy * xhat, axis=0, keepdims=True)
    grads_ref[1:2, :] = jnp.sum(dy, axis=0, keepdims=True)


def ln2(part, normed, keep, near, far, dy, gain, bias):
    rows, width = far.shape
    piece = pl.BlockSpec((rows, width), lambda i: (part, 0))
    first = full((rows, width))
    row = full((1, width))
    return pl.pallas_call(
        ln2_kernel,
        grid=(1,),
        out_shape=[
            jax.ShapeDtypeStruct((rows, width), BF),
            jax.ShapeDtypeStruct((rows, width), F32),
            jax.ShapeDtypeStruct((rows, width), BF),
            jax.ShapeDtypeStruct((2, width), F32),
        ],
        in_specs=[piece, first, first, first, piece, row, row],
        out_specs=[first, first, first, full((2, width))],
        compiler_params=params(),
        cost_estimate=cost(far.size * 20, far.size * 20),
        name="norm_two",
    )(normed, keep, near, far, dy, gain, bias)


def ln1_back_kernel(
    pre_ref, d2_ref, keep_ref, near_ref, far_ref, gain_ref, d_ref, low_ref, grads_ref
):
    grad = d2_ref[...] + (
        keep_ref[...].astype(F32) + near_ref[...].astype(F32) + far_ref[...].astype(F32)
    )
    xhat, r = centre(pre_ref[...])
    d = norm_back(xhat, r, gain_ref[...], grad)
    d_ref[...] = d
    low_ref[...] = d.astype(BF)
    grads_ref[0:1, :] = jnp.sum(grad * xhat, axis=0, keepdims=True)
    grads_ref[1:2, :] = jnp.sum(grad, axis=0, keepdims=True)


def ln1_back(part, pre, d2, keep, near, far, gain):
    rows, width = far.shape
    piece = pl.BlockSpec((rows, width), lambda i: (part, 0))
    first = full((rows, width))
    return pl.pallas_call(
        ln1_back_kernel,
        grid=(1,),
        out_shape=[
            jax.ShapeDtypeStruct((rows, width), F32),
            jax.ShapeDtypeStruct((rows, width), BF),
            jax.ShapeDtypeStruct((2, width), F32),
        ],
        in_specs=[piece, first, first, first, first, full((1, width))],
        out_specs=[first, first, full((2, width))],
        compiler_params=params(),
        cost_estimate=cost(far.size * 20, far.size * 20),
        name="norm_one_backward",
    )(pre, d2, keep, near, far, gain)


def swap(value, axis, bit):
    count = lax.axis_size(axis)
    return lax.ppermute(value, axis, [(i, i ^ bit) for i in range(count)])


def swap_chip_edges(value):
    count = lax.axis_size("seq") * lax.axis_size("tp")
    pairs = []
    for i in range(1, count - 1, 2):
        pairs += [(i, i + 1), (i + 1, i)]
    return lax.ppermute(value, ("seq", "tp"), pairs)


def shift_z(value, k):
    count = lax.axis_size("seq")
    return lax.ppermute(value, "seq", [(i, (i + 2 * k) % count) for i in range(count)])


def fold_kernel(place_ref, g_ref, r_ref, *out_refs):
    half = r_ref.shape[0]
    shard = out_refs[0].shape[0]
    base = place_ref[0] * half
    for k, out_ref in enumerate(out_refs):
        at = lax.rem(place_ref[1] + k, 4) * shard
        own = g_ref[pl.ds(pl.multiple_of(base + at, shard), shard), :].astype(F32)
        other = r_ref[pl.ds(pl.multiple_of(at, shard), shard), :].astype(F32)
        out_ref[...] = (own + other).astype(BF)


def fold(place, g, r):
    rows, width = r.shape
    vm = pl.BlockSpec(memory_space=pltpu.VMEM)
    return pl.pallas_call(
        fold_kernel,
        out_shape=[jax.ShapeDtypeStruct((rows // 4, width), BF)] * 4,
        in_specs=[smem(), vm, vm],
        out_specs=[vm] * 4,
        compiler_params=params(),
        cost_estimate=cost(r.size, r.size * 6),
        name="fold_half",
    )(place, g, r)


def spread_kernel(place_ref, *refs):
    out_ref = refs[-1]
    shard = refs[0].shape[0]
    for k, ref in enumerate(refs[:-1]):
        at = lax.rem(place_ref[1] + 4 - k, 4) * shard
        out_ref[pl.ds(pl.multiple_of(at, shard), shard), :] = ref[...]


def spread(place, shards):
    shard, width = shards[0].shape
    vm = pl.BlockSpec(memory_space=pltpu.VMEM)
    return pl.pallas_call(
        spread_kernel,
        out_shape=jax.ShapeDtypeStruct((4 * shard, width), BF),
        in_specs=[smem()] + [vm] * 4,
        out_specs=vm,
        compiler_params=params(),
        cost_estimate=cost(0, shard * width * 16),
        name="spread_shards",
    )(place, *shards)


def join_kernel(place_ref, own_ref, other_ref, out_ref):
    half = own_ref.shape[0]
    own = place_ref[0] * half
    out_ref[pl.ds(pl.multiple_of(own, half), half), :] = own_ref[...].astype(F32)
    out_ref[pl.ds(pl.multiple_of(half - own, half), half), :] = other_ref[...].astype(F32)


def join(place, own, other):
    half, width = own.shape
    vm = pl.BlockSpec(memory_space=pltpu.VMEM)
    return pl.pallas_call(
        join_kernel,
        out_shape=jax.ShapeDtypeStruct((2 * half, width), F32),
        in_specs=[smem(), vm, vm],
        out_specs=vm,
        compiler_params=params(),
        cost_estimate=cost(0, own.size * 12),
        name="join_halves",
    )(place, own, other)


def sum_over_seq(place, g):
    if lax.axis_size("seq") != 8:
        return lax.psum(g, "seq").astype(F32)
    half = g.shape[0] // 2
    sent = lax.dynamic_slice_in_dim(g, (1 - place[0]) * half, half, 0)
    shards = fold(place, g, swap(sent, "seq", 1))
    own = shards[0].astype(F32)
    for k in (1, 2, 3):
        own = own + shift_z(shards[k], k).astype(F32)
    own = own.astype(BF)
    whole = spread(place, [own] + [shift_z(own, k) for k in (1, 2, 3)])
    return join(place, whole, swap(whole, "seq", 1))


def sum_small(value):
    for bit in (1, 2):
        value = value + swap(value, "tp", bit)
    count = lax.axis_size("seq")
    bit = 1
    while bit < count:
        value = value + swap(value, "seq", bit)
        bit *= 2
    return value


def per_device(
    inputs, lengths, w_qkv, w_out, w_in, w_down, ln1_gain, ln1_bias, ln2_gain, ln2_bias, cotangent
):
    own_rows, width = inputs.shape
    tp_count = lax.axis_size("tp")
    head_width = w_qkv.shape[2]
    heads = head_width // HD
    chip_rows = 2 * own_rows
    tp = lax.axis_index("tp")
    seq = lax.axis_index("seq")
    core = tp & 1
    even = core == 0
    first = (seq * tp_count + 2 * (tp >> 1)) * own_rows
    place = jnp.stack([seq & 1, seq >> 1]).astype(jnp.int32)

    bounds = jnp.cumsum(lengths)[:, None]
    tokens = (first + jnp.arange(chip_rows, dtype=jnp.int32))[None, :]
    before = bounds <= tokens
    start = jnp.max(jnp.where(before, bounds, 0), axis=0)
    end = jnp.min(jnp.where(before, jnp.iinfo(jnp.int32).max, bounds), axis=0)
    se = jnp.stack([start, end]) - (first - QB)
    se = jnp.pad(se, ((0, 6), (0, 0)))
    table = jnp.asarray(slope_table(HEADS))
    slopes = lax.dynamic_slice_in_dim(table, tp * heads, heads)
    slopes_far = lax.dynamic_slice_in_dim(table, (tp ^ 2) * heads, heads)

    wt = w_qkv.transpose(0, 2, 1).reshape(3 * head_width, width)
    wt_far = swap(wt, "tp", 2)
    w_out_far = swap(w_out, "tp", 2)

    sibling = swap(inputs, "tp", 1)
    edge = swap_chip_edges(
        lax.dynamic_slice_in_dim(inputs, core * (own_rows - QB), QB, axis=0)
    )
    edge_sibling = swap(edge, "tp", 1)
    rows = jnp.concatenate(
        [
            jnp.where(even, edge, edge_sibling),
            jnp.where(even, inputs, sibling),
            jnp.where(even, sibling, inputs),
            jnp.where(even, edge_sibling, edge),
        ],
        axis=0,
    )

    wg, wu = w_in[:, 0], w_in[:, 1]
    wgt, wut, wdt = wg.T, wu.T, w_down.T

    def project(weights):
        natural = weights[head_width:].reshape(2 * heads, HD, width)
        natural = jnp.pad(natural, ((0, 0), (0, 128 - HD), (0, 0))).reshape(-1, width)
        return dot(weights, rows, 1, 1).astype(BF), dot(rows, natural, 1, 1).astype(BF)

    qkv, kv = project(wt)
    ctx = attn_fwd(heads, slopes, se, qkv, kv)
    qkv_far, kv_far = project(wt_far)
    ctx_far = attn_fwd(heads, slopes_far, se, qkv_far, kv_far)

    def attended_rows(which):
        at = which * own_rows
        near = lax.dynamic_slice_in_dim(ctx, at, own_rows, 1)
        far = lax.dynamic_slice_in_dim(ctx_far, at, own_rows, 1)
        return dot(near, w_out, 0, 0) + dot(far, w_out_far, 0, 0)

    attended_sent = swap(attended_rows(1 - core).astype(BF), "tp", 1)
    gain1, bias1 = ln1_gain[None], ln1_bias[None]
    gain2, bias2 = ln2_gain[None], ln2_bias[None]
    pre_one, normed, low = ln1(inputs, attended_rows(core), attended_sent, gain1, bias1)

    parts = 2
    piece = own_rows // parts

    def gather(value):
        pair = jnp.concatenate([value, swap(value, "tp", 2)], axis=0)
        return jnp.concatenate([pair, swap(pair, "tp", 1)], axis=0)

    def scatter(keep, sent):
        near = swap(sent, "tp", 1)
        far = (keep[piece:].astype(F32) + near[piece:].astype(F32)).astype(BF)
        return near, swap(far, "tp", 2)

    hidden_rows = [gather(low[p * piece : (p + 1) * piece]) for p in range(parts)]
    forward = [ff_fwd(hidden_rows[p], wg, wu, w_down) for p in range(parts)]
    second = []
    for p in range(parts):
        keep, sent = forward[p][3:]
        near, far = scatter(keep, sent)
        second.append(ln2(p, normed, keep, near, far, cotangent, gain2, bias2))
    layer_out = jnp.concatenate([s[0] for s in second], axis=0)
    d_branch = [gather(s[2]) for s in second]
    backward = [
        ff_bwd(d_branch[p], forward[p][1], forward[p][2], wdt, wgt, wut) for p in range(parts)
    ]
    grad_down = sum(dot(forward[p][0], d_branch[p], 0, 0) for p in range(parts)).astype(BF)
    grad_down = sum_over_seq(place, grad_down)
    first_back = []
    for p in range(parts):
        keep, sent = backward[p][2:]
        near, far = scatter(keep, sent)
        first_back.append(ln1_back(p, pre_one, second[p][1], keep, near, far, gain1))
    grad_gate = sum(dot(hidden_rows[p], backward[p][0], 0, 0) for p in range(parts))
    grad_up = sum(dot(hidden_rows[p], backward[p][1], 0, 0) for p in range(parts))
    grad_in = sum_over_seq(
        place, jnp.concatenate([grad_gate.astype(BF), grad_up.astype(BF)], axis=0)
    )
    grad_in = jnp.stack([grad_in[:width], grad_in[width:]], axis=1)
    norm_grads = sum_small(
        jnp.concatenate([sum(f[2] for f in first_back), sum(s[3] for s in second)], axis=0)
    )

    halves = [f[1] for f in first_back]
    halves_sibling = [swap(h, "tp", 1) for h in halves]
    d_attended = jnp.concatenate(
        [jnp.where(even, a, b) for a, b in zip(halves, halves_sibling)]
        + [jnp.where(even, b, a) for a, b in zip(halves, halves_sibling)],
        axis=0,
    )
    d_ctx_far = dot(w_out_far, d_attended, 1, 1).astype(BF)
    d_qkv_far = attn_bwd(heads, slopes_far, se, qkv_far, kv_far, d_ctx_far)
    far_grads = swap(
        jnp.concatenate(
            [dot(d_qkv_far, rows, 1, 0).astype(BF), dot(ctx_far, d_attended, 1, 0).astype(BF)],
            axis=0,
        ),
        "tp",
        2,
    )
    d_ctx = dot(w_out, d_attended, 1, 1).astype(BF)
    d_qkv = attn_bwd(heads, slopes, se, qkv, kv, d_ctx)
    own_grads = jnp.concatenate(
        [dot(d_qkv, rows, 1, 0), dot(ctx, d_attended, 1, 0)], axis=0
    )
    grad_attn = sum_over_seq(place, (own_grads + far_grads.astype(F32)).astype(BF))
    grad_qkv = grad_attn[: 3 * head_width].reshape(3, head_width, width).transpose(0, 2, 1)
    grad_out = grad_attn[3 * head_width :]

    half = own_rows + QB

    def window_half(which):
        at = which * half
        near = lax.dynamic_slice_in_dim(d_qkv, at, half, 1)
        far = lax.dynamic_slice_in_dim(d_qkv_far, at, half, 1)
        return dot(near, wt, 0, 0) + dot(far, wt_far, 0, 0)

    from_sibling = swap(window_half(1 - core).astype(BF), "tp", 1)
    d_half = window_half(core) + from_sibling.astype(F32)
    d_edge = swap_chip_edges(
        lax.dynamic_slice_in_dim(d_half, core * own_rows, QB, 0).astype(BF)
    )
    d_pre_one = jnp.concatenate([f[0] for f in first_back], axis=0)
    grad_input = d_pre_one + lax.dynamic_slice_in_dim(d_half, (1 - core) * QB, own_rows, 0)
    zeros = jnp.zeros((own_rows - QB, width), F32)
    d_edge = d_edge.astype(F32)
    grad_input = grad_input + jnp.where(
        even, jnp.concatenate([d_edge, zeros]), jnp.concatenate([zeros, d_edge])
    )
    return (
        layer_out,
        grad_input,
        grad_qkv,
        grad_out,
        grad_in,
        grad_down,
        norm_grads[0],
        norm_grads[1],
        norm_grads[2],
        norm_grads[3],
    )


def solution(mesh):
    in_specs = (
        P(("seq", "tp"), None),
        P(),
        P(None, None, "tp"),
        P("tp", None),
        P(None, None, "tp"),
        P("tp", None),
        P(),
        P(),
        P(),
        P(),
        P(("seq", "tp"), None),
    )
    out_specs = (
        P(("seq", "tp"), None),
        P(("seq", "tp"), None),
        P(None, None, "tp"),
        P("tp", None),
        P(None, None, "tp"),
        P("tp", None),
        P(),
        P(),
        P(),
        P(),
    )
    return jax.shard_map(
        per_device, mesh=mesh, in_specs=in_specs, out_specs=out_specs, check_vma=False
    )
```

time: 872 us -> 329 us (0.38)
  waiting for transfers between devices: 461 us -> 100 us
  local copies, waits for them, and re-layouts: 199 us -> 51.9 us
  Pallas kernels: 0 us -> 60.9 us
  matrix products: 86 us -> 26.7 us
  starting transfers between devices: 13.9 us -> 73 us
  blocking collectives: 43.6 us -> 0 us
  other arithmetic: 46 us -> 8.54 us
  between operations: 15.3 us -> 2.41 us
    psum x1 -> x0, waiting for transfers between devices: 271 us -> none  [per_device(): lax.psum((grad_qkv, grad_out, grad_in, grad_down), 'seq')]
    gather x16 -> x0, local copies, waits for them, and re-layouts: 163 us -> none  [sequence_ids(): located = jnp.searchsorted(bounds, places, side='right')]
    reduce_scatter x4 -> x0, waiting for transfers between devices: 117 us -> none  [the longest x1 50.3 us: per_device(): lax.psum_scatter(jnp.dot(context, w_out, preferred_element_type=jnp.float...]
    ppermute x4 -> x56, waiting for transfers between devices: 0.71 us -> 100 us  [the longest x36 53.8 us: swap(): return lax.ppermute(value, axis, [(i, i ^ bit) for i in range(count)])]
    all_gather x4 -> x0, waiting for transfers between devices: 72 us -> none  [the longest x1 24.2 us: per_device(): lax.all_gather(d_pre_two.astype(jnp.bfloat16), 'tp', axis=0, tiled=True)]
    pallas_call x0 -> x22, Pallas kernels: none -> 60.9 us  [the longest x2 18.9 us: attn_bwd(): pl.pallas_call(functools.partial(attn_bwd_kernel, heads), out_shape=jax.S...]
    ppermute x4 -> x56, starting transfers between devices: 13.1 us -> 73 us  [the longest x18 40.1 us: shift_z(): lax.ppermute(value, 'seq', [(i, (i + 2 * k) % count) for i in range(count)])]
    dot_general x32 -> x24, matrix products: 84.9 us -> 26.7 us  [dot(): lax.dot_general(a, b, (((ca,), (cb,)), ((), ())), preferred_element_type=...]
  transfers between devices with their start and end apart: 13 -> 56, of which waited for: 8 -> 24; matrix products, arithmetic and copies ran while one was open for 23% -> 21% of each run, Pallas kernels for 0% -> 18%
where the time goes in v1:
time: 329 us; the launch traced here: 324 us
  waiting for transfers between devices  100 us (30%)
  starting transfers between devices  73 us (22%)
  Pallas kernels  60.9 us (19%)
  local copies, waits for them, and re-layouts  51.9 us (16%)
  matrix products  26.7 us (8%)
  other arithmetic  8.54 us (3%)
    ppermute x36, waiting for transfers between devices, swap(): return lax.ppermute(value, axis, [(i, i ^ bit) for i in range(count)])  53.8 us
    ppermute x18, waiting for transfers between devices, shift_z(): lax.ppermute(value, 'seq', [(i, (i + 2 * k) % count) for i in range(count)])  46.3 us
    ppermute x18, starting transfers between devices, shift_z(): lax.ppermute(value, 'seq', [(i, (i + 2 * k) % count) for i in range(count)])  40.1 us
    unnamed x164, local copies, waits for them, and re-layouts  39.5 us
    ppermute x36, starting transfers between devices, swap(): return lax.ppermute(value, axis, [(i, i ^ bit) for i in range(count)])  31.6 us
    dot_general x24, matrix products, dot(): lax.dot_general(a, b, (((ca,), (cb,)), ((), ())), preferred_element_type=...  26.7 us
    pallas_call x2, Pallas kernels, attn_bwd(): pl.pallas_call(functools.partial(attn_bwd_kernel, heads), out_shape=jax.S...  18.9 us
    pallas_call x2, Pallas kernels, attn_fwd(): pl.pallas_call(functools.partial(attn_fwd_kernel, heads), out_shape=jax.S...  13.4 us
  transfers between devices with their start and end apart: 56, of which 24 were waited for; matrix products, arithmetic and copies ran while one was open for 21% of the time, Pallas kernels for 18%

profile of v1, /device:TPU:0, one launch (start us, length us, event | category | flops | bytes accessed | tf_op | source)
XLA Modules:
  0.0 323.6 jit_solution(16745457585742354197)
XLA Ops:
  2.8 3.9 %collective-permute-start.4 = (bf16[192,768]{1,0:T(8,128)(2,1)}, bf16[192,768]{1,0:T(8,128)(2,1)S(1)}, u32[]{:S(2)}, u32[]{:S(2)}) collective-permute-start(bf16[192,768]{1,0:T(8,128)(2,1)} %param.15), channel_id=1, source_target_pairs={{0,2},{1,3},{2,0},{3,1},{4,6},{5,7},{6,4},{7,5},{8,10},{9,11},{10,... | collective-permute-start | bytes 884744 | tf_op jit(solution)/shard_map/ppermute | solution.py:360
  8.3 4.3 %collective-permute-start.1 = (bf16[128,768]{1,0:T(8,128)(2,1)S(1)}, bf16[128,768]{1,0:T(8,128)(2,1)S(1)}, u32[]{:S(2)}, u32[]{:S(2)}) collective-permute-start(bf16[128,768]{1,0:T(8,128)(2,1)S(1)} %collective-permute-done), channel_id=1, source_target_pairs={{0,1},{1,0},{2,3},{3,2},{4,5},{5,4},{6,7},{7,6},{8,9},{9,8},{10,11... | collective-permute-start | bytes 589832 | tf_op jit(solution)/shard_map/ppermute | solution.py:360
  15.2 1.5 copy-done.45
  17.9 1.4 convolution_convert_fusion.1.kv_ref
  19.4 6.8 %attention_forward.2 = bf16[192,768]{1,0:T(8,128)(2,1)S(1)} custom-call(f32[3]{0:T(128)S(1)} %get-tuple-element.155.slopes_ref, s32[8,768]{1,0:T(8,128)S(1)} %pad.17.se_ref, bf16[576,1024]{1,0:T(8,128)(2,1)S(1)} %fusion.1.qkv_ref, bf16[1024,768]{1,0:T(8,128)(2,1)S(1)} %convolution_convert_fusion.1.kv_ref), custom_call_target="tpu_custom_call" | custom-call | flops 905969664 | bytes 2752512 | tf_op jit(solution)/shard_map/attention_forward/pallas_call | solution.py:87
  26.6 9.0 %collective-permute-done.3 = bf16[576,768]{1,0:T(8,128)(2,1)} collective-permute-done((bf16[576,768]{1,0:T(8,128)(2,1)}, bf16[576,768]{1,0:T(8,128)(2,1)}, u32[]{:S(2)}, u32[]{:S(2)}) %collective-permute-start.3) | collective-permute-done | bytes 884768 | tf_op jit(solution)/shard_map/ppermute | solution.py:360
  36.8 1.4 convolution_convert_fusion.kv_ref
  38.3 2.8 fusion.2.qkv_ref
  41.2 6.6 %attention_forward.3 = bf16[192,768]{1,0:T(8,128)(2,1)S(1)} custom-call(f32[3]{0:T(128)S(1)} %get-tuple-element.154.slopes_ref, s32[8,768]{1,0:T(8,128)S(1)} %pad.17.se_ref, bf16[576,1024]{1,0:T(8,128)(2,1)S(1)} %fusion.2.qkv_ref, bf16[1024,768]{1,0:T(8,128)(2,1)S(1)} %convolution_convert_fusion.kv_ref), custom_call_target="tpu_custom_call" | custom-call | flops 905969664 | bytes 2752512 | tf_op jit(solution)/shard_map/attention_forward/pallas_call | solution.py:87
  50.9 1.3 fusion.21
  53.3 2.3 collective-permute-start.10
  55.7 7.8 %collective-permute-done.10 = bf16[192,768]{1,0:T(8,128)(2,1)S(1)} collective-permute-done((bf16[192,768]{1,0:T(8,128)(2,1)S(1)}, bf16[192,768]{1,0:T(8,128)(2,1)S(1)}, u32[]{:S(2)}, u32[]{:S(2)}) %collective-permute-start.10) | collective-permute-done | bytes 294944 | tf_op jit(solution)/shard_map/ppermute | solution.py:360
  63.6 3.4 %fusion.36 = (bf16[768,1,768]{2,1,0:T(2,128)(2,1)S(1)}, bf16[768,1,768]{2,1,0:T(2,128)(2,1)S(1)}) fusion(bf16[768,2,768]{2,1,0:T(2,128)(2,1)S(1)} %copy-done.44), kind=kLoop, calls=%fused_computation.109 | loop fusion | bytes 4718592 | tf_op jit(solution)/shard_map/slice | solution.py:514
  67.0 2.5 collective-permute-done.6
  70.1 1.3 copy-done.6
  71.5 4.1 %ff_forward.3 = (bf16[768,768]{1,0:T(8,128)(2,1)S(1)}, bf16[768,768]{1,0:T(8,128)(2,1)S(1)}, bf16[768,768]{1,0:T(8,128)(2,1)S(1)}, bf16[384,768]{1,0:T(8,128)(2,1)S(1)}, bf16[384,768]{1,0:T(8,128)(2,1)S(1)}) custom-call(bf16[768,768]{1,0:T(8,128)(2,1)S(1)} %pad_maximum_fusion.4.x_ref, bf16[768,768]{1,0:T(8,128)(2,1)S(1)} %get-tuple-element.157.wg_ref, ...), custom_call_target="tpu_custom_call" | custom-call | flops 2717908992 | bytes 7077888 | tf_op jit(solution)/shard_map/ff_forward/pallas_call | solution.py:185
  80.1 4.2 %ff_forward.2 = (bf16[768,768]{1,0:T(8,128)(2,1)S(1)}, bf16[768,768]{1,0:T(8,128)(2,1)S(1)}, bf16[768,768]{1,0:T(8,128)(2,1)S(1)}, bf16[384,768]{1,0:T(8,128)(2,1)S(1)}, bf16[384,768]{1,0:T(8,128)(2,1)S(1)}) custom-call(bf16[768,768]{1,0:T(8,128)(2,1)S(1)} %pad_maximum_fusion.3.x_ref, bf16[768,768]{1,0:T(8,128)(2,1)S(1)} %get-tuple-element.157.wg_ref, ...), custom_call_target="tpu_custom_call" | custom-call | flops 2717908992 | bytes 7077888 | tf_op jit(solution)/shard_map/ff_forward/pallas_call | solution.py:185
  86.5 1.8 collective-permute-start.13
  90.0 1.7 collective-permute-start.9
  91.8 4.6 %collective-permute-done.13.far_ref = bf16[192,768]{1,0:T(8,128)(2,1)S(1)} collective-permute-done((bf16[192,768]{1,0:T(8,128)(2,1)S(1)}, bf16[192,768]{1,0:T(8,128)(2,1)S(1)}, u32[]{:S(2)}, u32[]{:S(2)}) %collective-permute-start.13) | collective-permute-done | bytes 294944 | tf_op jit(solution)/shard_map/ppermute | solution.py:360
  96.4 1.3 norm_two.3
  99.8 1.7 collective-permute-start.18
  101.5 2.8 copy.44
  104.4 6.4 %copy.46 = bf16[768,1,768]{0,2,1:T(8,128)(2,1)} copy(bf16[768,1,768]{2,1,0:T(2,128)(2,1)} %copy-done.43) | data formatting | bytes 2359296
  110.8 6.4 %copy.47 = bf16[768,1,768]{0,2,1:T(8,128)(2,1)} copy(bf16[768,1,768]{2,1,0:T(2,128)(2,1)} %copy-done.42) | data formatting | bytes 2359296
  118.3 1.5 norm_two.2
  122.7 5.2 %collective-permute-done.14 = bf16[192,768]{1,0:T(8,128)(2,1)S(1)} collective-permute-done((bf16[192,768]{1,0:T(8,128)(2,1)S(1)}, bf16[192,768]{1,0:T(8,128)(2,1)S(1)}, u32[]{:S(2)}, u32[]{:S(2)}) %collective-permute-start.14) | collective-permute-done | bytes 294944 | tf_op jit(solution)/shard_map/ppermute | solution.py:360
  129.2 4.1 %ff_backward.3 = (bf16[768,768]{1,0:T(8,128)(2,1)S(1)}, bf16[768,768]{1,0:T(8,128)(2,1)S(1)}, bf16[384,768]{1,0:T(8,128)(2,1)S(1)}, bf16[384,768]{1,0:T(8,128)(2,1)S(1)}) custom-call(bf16[768,768]{1,0:T(8,128)(2,1)S(1)} %constant_dynamic-update-slice_fusion.3.db_ref, bf16[768,768]{1,0:T(8,128)(2,1)S(1)} %copy-done.39, bf16[768,768]{1,0:T(8,128)(2,1)S(1)} %copy-done.41, ...), custom_call_target="tpu_custom_call" | custom-call | flops 2717908992 | bytes 7077888 | tf_op jit(solution)/shard_map/ff_backward/pallas_call | solution.py:226
  133.9 4.1 %ff_backward.2 = (bf16[768,768]{1,0:T(8,128)(2,1)S(1)}, bf16[768,768]{1,0:T(8,128)(2,1)S(1)}, bf16[384,768]{1,0:T(8,128)(2,1)S(1)}, bf16[384,768]{1,0:T(8,128)(2,1)S(1)}) custom-call(bf16[768,768]{1,0:T(8,128)(2,1)S(1)} %constant_dynamic-update-slice_fusion.db_ref, bf16[768,768]{1,0:T(8,128)(2,1)S(1)} %copy-done.35, bf16[768,768]{1,0:T(8,128)(2,1)S(1)} %copy-done.37, ...), custom_call_target="tpu_custom_call" | custom-call | flops 2717908992 | bytes 7077888 | tf_op jit(solution)/shard_map/ff_backward/pallas_call | solution.py:226
  140.6 1.6 collective-permute-start.43
  144.6 1.6 collective-permute-start.21
  148.0 6.6 %collective-permute-done.21.far_ref = bf16[192,768]{1,0:T(8,128)(2,1)S(1)} collective-permute-done((bf16[192,768]{1,0:T(8,128)(2,1)S(1)}, bf16[192,768]{1,0:T(8,128)(2,1)S(1)}, u32[]{:S(2)}, u32[]{:S(2)}) %collective-permute-start.21) | collective-permute-done | bytes 294944 | tf_op jit(solution)/shard_map/ppermute | solution.py:360
  155.1 5.0 %collective-permute-done.17.far_ref = bf16[192,768]{1,0:T(8,128)(2,1)S(1)} collective-permute-done((bf16[192,768]{1,0:T(8,128)(2,1)S(1)}, bf16[192,768]{1,0:T(8,128)(2,1)S(1)}, u32[]{:S(2)}, u32[]{:S(2)}) %collective-permute-start.17) | collective-permute-done | bytes 294944 | tf_op jit(solution)/shard_map/ppermute | solution.py:360
  162.7 3.4 %collective-permute-start.46 = (bf16[96,768]{1,0:T(8,128)(2,1)S(1)}, bf16[96,768]{1,0:T(8,128)(2,1)S(1)}, u32[]{:S(2)}, u32[]{:S(2)}) collective-permute-start(bf16[96,768]{1,0:T(8,128)(2,1)S(1)} %get-tuple-element.99), channel_id=1, source_target_pairs={{0,24},{4,28},{8,0},{12,4},{16,8},{20,12},{24,16},{28,20},{1,25},{... | collective-permute-start | bytes 442376 | tf_op jit(solution)/shard_map/ppermute | solution.py:373
  167.4 1.6 collective-permute-start.52
  169.2 2.0 collective-permute-done.52
  171.7 1.6 fusion.4
  173.3 1.5 collective-permute-done.53
  175.5 4.0 %collective-permute-done.45 = bf16[96,768]{1,0:T(8,128)(2,1)S(1)} collective-permute-done((bf16[96,768]{1,0:T(8,128)(2,1)S(1)}, bf16[96,768]{1,0:T(8,128)(2,1)S(1)}, u32[]{:S(2)}, u32[]{:S(2)}) %collective-permute-start.45) | collective-permute-done | bytes 147488 | tf_op jit(solution)/shard_map/ppermute | solution.py:373
  179.6 2.2 collective-permute-start.47
  181.8 1.4 collective-permute-done.54
  186.1 9.5 %attention_backward.3 = bf16[576,1024]{1,0:T(8,128)(2,1)S(1)} custom-call(f32[3]{0:T(128)S(1)} %copy-done.21, s32[8,768]{1,0:T(8,128)S(1)} %copy-done.17, bf16[576,1024]{1,0:T(8,128)(2,1)S(1)} %copy-done.29, bf16[1024,768]{1,0:T(8,128)(2,1)S(1)} %copy-done.25, bf16[192,768]{1,0:T(8,128)(2,1)S(1)} %fusion.7.dctx_ref), custom_call_target="tpu_custom_call" | custom-call | flops 2264924160 | bytes 3932160 | tf_op jit(solution)/shard_map/attention_backward/pallas_call | solution.py:134
  196.8 1.6 collective-permute-start.26
  199.0 9.5 %attention_backward.2 = bf16[576,1024]{1,0:T(8,128)(2,1)S(1)} custom-call(f32[3]{0:T(128)S(1)} %get-tuple-element.155.slopes_ref, s32[8,768]{1,0:T(8,128)S(1)} %copy-done.17, bf16[576,1024]{1,0:T(8,128)(2,1)S(1)} %copy-done.27, bf16[1024,768]{1,0:T(8,128)(2,1)S(1)} %copy-done.23, bf16[192,768]{1,0:T(8,128)(2,1)S(1)} %fusion.6.dctx_ref), custom_call_target="tpu_custom_call" | custom-call | flops 2264924160 | bytes 3932160 | tf_op jit(solution)/shard_map/attention_backward/pallas_call | solution.py:134
  209.3 1.4 collective-permute-start.38
  213.8 2.0 add_convert_fusion.3
  215.8 2.4 collective-permute-done.38
  218.2 14.4 %collective-permute-start.48 = (bf16[96,768]{1,0:T(8,128)(2,1)S(1)}, bf16[96,768]{1,0:T(8,128)(2,1)S(1)}, u32[]{:S(2)}, u32[]{:S(2)}) collective-permute-start(bf16[96,768]{1,0:T(8,128)(2,1)S(1)} %add_convert_fusion.9.refs_0_), channel_id=1, source_target_pairs={{0,16},{4,20},{8,24},{12,28},{16,0},{20,4},{24,8},{28,12},{1,17},{... | collective-permute-start | bytes 442376 | tf_op jit(solution)/shard_map/ppermute | solution.py:373
  232.5 8.4 %collective-permute-done.37 = bf16[192,768]{1,0:T(8,128)(2,1)S(1)} collective-permute-done((bf16[192,768]{1,0:T(8,128)(2,1)S(1)}, bf16[192,768]{1,0:T(8,128)(2,1)S(1)}, u32[]{:S(2)}, u32[]{:S(2)}) %collective-permute-start.37) | collective-permute-done | bytes 294944 | tf_op jit(solution)/shard_map/ppermute | solution.py:373
  240.9 1.6 collective-permute-start.55
  243.7 2.8 collective-permute-start.40
  246.5 1.3 collective-permute-start.41
  250.6 4.3 %collective-permute-done.39.refs_1_ = bf16[192,768]{1,0:T(8,128)(2,1)S(1)} collective-permute-done((bf16[192,768]{1,0:T(8,128)(2,1)S(1)}, bf16[192,768]{1,0:T(8,128)(2,1)S(1)}, u32[]{:S(2)}, u32[]{:S(2)}) %collective-permute-start.39) | collective-permute-done | bytes 294944 | tf_op jit(solution)/shard_map/ppermute | solution.py:373
  255.5 11.5 %collective-permute-done.40.refs_2_ = bf16[192,768]{1,0:T(8,128)(2,1)S(1)} collective-permute-done((bf16[192,768]{1,0:T(8,128)(2,1)S(1)}, bf16[192,768]{1,0:T(8,128)(2,1)S(1)}, u32[]{:S(2)}, u32[]{:S(2)}) %collective-permute-start.40) | collective-permute-done | bytes 294944 | tf_op jit(solution)/shard_map/ppermute | solution.py:373
  268.2 2.0 fusion.11
  270.9 6.8 %collective-permute-start.30 = (bf16[96,768]{1,0:T(8,128)(2,1)S(1)}, bf16[96,768]{1,0:T(8,128)(2,1)S(1)}, u32[]{:S(2)}, u32[]{:S(2)}) collective-permute-start(bf16[96,768]{1,0:T(8,128)(2,1)S(1)} %get-tuple-element.85), channel_id=1, source_target_pairs={{0,24},{4,28},{8,0},{12,4},{16,8},{20,12},{24,16},{28,20},{1,25},{... | collective-permute-start | bytes 442376 | tf_op jit(solution)/shard_map/ppermute | solution.py:373
  279.2 2.8 collective-permute-done.30
  282.7 8.8 %collective-permute-done.29 = bf16[96,768]{1,0:T(8,128)(2,1)S(1)} collective-permute-done((bf16[96,768]{1,0:T(8,128)(2,1)S(1)}, bf16[96,768]{1,0:T(8,128)(2,1)S(1)}, u32[]{:S(2)}, u32[]{:S(2)}) %collective-permute-start.29) | collective-permute-done | bytes 147488 | tf_op jit(solution)/shard_map/ppermute | solution.py:373
  292.7 3.1 collective-permute-start.33
  296.4 2.1 join_halves.5
  301.3 3.2 collective-permute-done.32.refs_2_
  307.2 5.8 %copy.45 = f32[768,2,768]{2,1,0:T(2,128)} copy(f32[768,2,768]{2,0,1:T(8,128)S(1)} %pad_maximum_fusion) | data formatting | bytes 9437184
  313.0 7.4 %collective-permute-done.34.other_ref = bf16[384,768]{1,0:T(8,128)(2,1)S(1)} collective-permute-done((bf16[384,768]{1,0:T(8,128)(2,1)S(1)}, bf16[384,768]{1,0:T(8,128)(2,1)S(1)}, u32[]{:S(2)}, u32[]{:S(2)}) %collective-permute-start.34) | collective-permute-done | bytes 589856 | tf_op jit(solution)/shard_map/ppermute | solution.py:360
  321.1 1.3 slice.108
  (327 shorter events, 68.6 us)
Async XLA Ops:
  0.6 14.4 %collective-permute-start.2 = (bf16[384,768]{1,0:T(8,128)(2,1)}, bf16[384,768]{1,0:T(8,128)(2,1)S(1)}, u32[]{:S(2)}, u32[]{:S(2)}) collective-permute-start(bf16[384,768]{1,0:T(8,128)(2,1)} %x_ref.1), channel_id=1, source_target_pairs={{0,1},{1,0},{2,3},{3,2},{4,5},{5,4},{6,7},{7,6},{8,9},{9,8},{10,11... | collective-permute-start | bytes 1769480 | tf_op jit(solution)/shard_map/ppermute | solution.py:360
  2.1 6.2 %collective-permute-start = (bf16[128,768]{1,0:T(8,128)(2,1)S(1)}, bf16[128,768]{1,0:T(8,128)(2,1)S(1)}, u32[]{:S(2)}, u32[]{:S(2)}) collective-permute-start(bf16[128,768]{1,0:T(8,128)(2,1)S(1)} %constant_dynamic-slice_fusion.2), channel_id=1, source_target_pairs={{1,2},{2,1},{3,4},{4,3},{5,6},{6,5},{7,8},{8,7},{9,10},{10,9},{11,... | collective-permute-start | bytes 589832 | tf_op jit(solution)/shard_map/ppermute | solution.py:368
  2.8 45.0 %collective-permute-start.4 = (bf16[192,768]{1,0:T(8,128)(2,1)}, bf16[192,768]{1,0:T(8,128)(2,1)S(1)}, u32[]{:S(2)}, u32[]{:S(2)}) collective-permute-start(bf16[192,768]{1,0:T(8,128)(2,1)} %param.15), channel_id=1, source_target_pairs={{0,2},{1,3},{2,0},{3,1},{4,6},{5,7},{6,4},{7,5},{8,10},{9,11},{10,... | collective-permute-start | bytes 884744 | tf_op jit(solution)/shard_map/ppermute | solution.py:360
  6.7 28.9 %collective-permute-start.3 = (bf16[576,768]{1,0:T(8,128)(2,1)}, bf16[576,768]{1,0:T(8,128)(2,1)}, u32[]{:S(2)}, u32[]{:S(2)}) collective-permute-start(bf16[576,768]{1,0:T(8,128)(2,1)} %bitcast.72), channel_id=1, source_target_pairs={{0,2},{1,3},{2,0},{3,1},{4,6},{5,7},{6,4},{7,5},{8,10},{9,11},{10,... | collective-permute-start | bytes 2654216 | tf_op jit(solution)/shard_map/ppermute | solution.py:360
  8.3 6.7 %collective-permute-start.1 = (bf16[128,768]{1,0:T(8,128)(2,1)S(1)}, bf16[128,768]{1,0:T(8,128)(2,1)S(1)}, u32[]{:S(2)}, u32[]{:S(2)}) collective-permute-start(bf16[128,768]{1,0:T(8,128)(2,1)S(1)} %collective-permute-done), channel_id=1, source_target_pairs={{0,1},{1,0},{2,3},{3,2},{4,5},{5,4},{6,7},{7,6},{8,9},{9,8},{10,11... | collective-permute-start | bytes 589832 | tf_op jit(solution)/shard_map/ppermute | solution.py:360
  12.7 28.5 %copy-start.16 = (s32[8,768]{1,0:T(8,128)}, s32[8,768]{1,0:T(8,128)S(1)}, u32[]{:S(2)}) copy-start(s32[8,768]{1,0:T(8,128)S(1)} %pad.17.se_ref) | copy-start | bytes 73732
  15.0 26.2 %copy-start.20 = (f32[3]{0:T(128)}, f32[3]{0:T(128)S(1)}, u32[]{:S(2)}) copy-start(f32[3]{0:T(128)S(1)} %get-tuple-element.154.slopes_ref) | copy-start | bytes 40
  15.0 23.2 %copy-start.69 = (bf16[128,768]{1,0:T(8,128)(2,1)}, bf16[128,768]{1,0:T(8,128)(2,1)S(1)}, u32[]{:S(2)}) copy-start(bf16[128,768]{1,0:T(8,128)(2,1)S(1)} %get-tuple-element.152) | copy-start | bytes 589828
  15.0 23.2 %copy-start.71 = (bf16[128,768]{1,0:T(8,128)(2,1)}, bf16[128,768]{1,0:T(8,128)(2,1)S(1)}, u32[]{:S(2)}) copy-start(bf16[128,768]{1,0:T(8,128)(2,1)S(1)} %get-tuple-element.153) | copy-start | bytes 589828
  15.1 23.1 %copy-start.61 = (bf16[384,768]{1,0:T(8,128)(2,1)}, bf16[384,768]{1,0:T(8,128)(2,1)S(1)}, u32[]{:S(2)}) copy-start(bf16[384,768]{1,0:T(8,128)(2,1)S(1)} %get-tuple-element.144) | copy-start | bytes 1769476
  15.2 23.1 %copy-start.63 = (bf16[384,768]{1,0:T(8,128)(2,1)}, bf16[384,768]{1,0:T(8,128)(2,1)S(1)}, u32[]{:S(2)}) copy-start(bf16[384,768]{1,0:T(8,128)(2,1)S(1)} %get-tuple-element.145) | copy-start | bytes 1769476
  26.2 24.7 %copy-start.10 = (bf16[192,768]{1,0:T(8,128)(2,1)}, bf16[192,768]{1,0:T(8,128)(2,1)S(1)}, u32[]{:S(2)}) copy-start(bf16[192,768]{1,0:T(8,128)(2,1)S(1)} %attention_forward.2) | copy-start | bytes 884740
  49.7 3.0 collective-permute-start.5
  53.3 25.8 %copy-start.47 = (bf16[192,768]{1,0:T(8,128)(2,1)}, bf16[192,768]{1,0:T(8,128)(2,1)S(1)}, u32[]{:S(2)}) copy-start(bf16[192,768]{1,0:T(8,128)(2,1)S(1)} %get-tuple-element.150) | copy-start | bytes 884740
  53.3 10.1 %collective-permute-start.10 = (bf16[192,768]{1,0:T(8,128)(2,1)S(1)}, bf16[192,768]{1,0:T(8,128)(2,1)S(1)}, u32[]{:S(2)}, u32[]{:S(2)}) collective-permute-start(bf16[192,768]{1,0:T(8,128)(2,1)S(1)} %get-tuple-element.151), channel_id=1, source_target_pairs={{0,2},{1,3},{2,0},{3,1},{4,6},{5,7},{6,4},{7,5},{8,10},{9,11},{10,... | collective-permute-start | bytes 884744 | tf_op jit(solution)/shard_map/ppermute | solution.py:360
  55.6 13.9 %collective-permute-start.6 = (bf16[192,768]{1,0:T(8,128)(2,1)S(1)}, bf16[192,768]{1,0:T(8,128)(2,1)S(1)}, u32[]{:S(2)}, u32[]{:S(2)}) collective-permute-start(bf16[192,768]{1,0:T(8,128)(2,1)S(1)} %get-tuple-element.150), channel_id=1, source_target_pairs={{0,2},{1,3},{2,0},{3,1},{4,6},{5,7},{6,4},{7,5},{8,10},{9,11},{10,... | collective-permute-start | bytes 884744 | tf_op jit(solution)/shard_map/ppermute | solution.py:360
  63.5 6.5 %collective-permute-start.11 = (bf16[384,768]{1,0:T(8,128)(2,1)S(1)}, bf16[384,768]{1,0:T(8,128)(2,1)S(1)}, u32[]{:S(2)}, u32[]{:S(2)}) collective-permute-start(bf16[384,768]{1,0:T(8,128)(2,1)S(1)} %pad_maximum_fusion.8), channel_id=1, source_target_pairs={{0,1},{1,0},{2,3},{3,2},{4,5},{5,4},{6,7},{7,6},{8,9},{9,8},{10,11... | collective-permute-start | bytes 1769480 | tf_op jit(solution)/shard_map/ppermute | solution.py:360
  69.5 9.7 %collective-permute-start.7 = (bf16[384,768]{1,0:T(8,128)(2,1)S(1)}, bf16[384,768]{1,0:T(8,128)(2,1)S(1)}, u32[]{:S(2)}, u32[]{:S(2)}) collective-permute-start(bf16[384,768]{1,0:T(8,128)(2,1)S(1)} %pad_maximum_fusion.7), channel_id=1, source_target_pairs={{0,1},{1,0},{2,3},{3,2},{4,5},{5,4},{6,7},{7,6},{8,9},{9,8},{10,11... | collective-permute-start | bytes 1769480 | tf_op jit(solution)/shard_map/ppermute | solution.py:360
  78.7 7.8 %collective-permute-start.12 = (bf16[384,768]{1,0:T(8,128)(2,1)S(1)}, bf16[384,768]{1,0:T(8,128)(2,1)S(1)}, u32[]{:S(2)}, u32[]{:S(2)}) collective-permute-start(bf16[384,768]{1,0:T(8,128)(2,1)S(1)} %get-tuple-element.63), channel_id=1, source_target_pairs={{0,1},{1,0},{2,3},{3,2},{4,5},{5,4},{6,7},{7,6},{8,9},{9,8},{10,11... | collective-permute-start | bytes 1769480 | tf_op jit(solution)/shard_map/ppermute | solution.py:360
  86.4 2.0 collective-permute-start.8
  86.5 9.9 %collective-permute-start.13 = (bf16[192,768]{1,0:T(8,128)(2,1)S(1)}, bf16[192,768]{1,0:T(8,128)(2,1)S(1)}, u32[]{:S(2)}, u32[]{:S(2)}) collective-permute-start(bf16[192,768]{1,0:T(8,128)(2,1)S(1)} %add_convert_fusion.7), channel_id=1, source_target_pairs={{0,2},{1,3},{2,0},{3,1},{4,6},{5,7},{6,4},{7,5},{8,10},{9,11},{10,... | collective-permute-start | bytes 884744 | tf_op jit(solution)/shard_map/ppermute | solution.py:360
  90.0 27.2 %collective-permute-start.9 = (bf16[192,768]{1,0:T(8,128)(2,1)}, bf16[192,768]{1,0:T(8,128)(2,1)}, u32[]{:S(2)}, u32[]{:S(2)}) collective-permute-start(bf16[192,768]{1,0:T(8,128)(2,1)} %add_convert_fusion.8), channel_id=1, source_target_pairs={{0,2},{1,3},{2,0},{3,1},{4,6},{5,7},{6,4},{7,5},{8,10},{9,11},{10,... | collective-permute-start | bytes 884744 | tf_op jit(solution)/shard_map/ppermute | solution.py:360
  99.8 20.4 %collective-permute-start.18 = (bf16[192,768]{1,0:T(8,128)(2,1)}, bf16[192,768]{1,0:T(8,128)(2,1)}, u32[]{:S(2)}, u32[]{:S(2)}) collective-permute-start(bf16[192,768]{1,0:T(8,128)(2,1)} %get-tuple-element.74), channel_id=1, source_target_pairs={{0,2},{1,3},{2,0},{3,1},{4,6},{5,7},{6,4},{7,5},{8,10},{9,11},{10,... | collective-permute-start | bytes 884744 | tf_op jit(solution)/shard_map/ppermute | solution.py:360
  119.9 8.0 %collective-permute-start.14 = (bf16[192,768]{1,0:T(8,128)(2,1)S(1)}, bf16[192,768]{1,0:T(8,128)(2,1)S(1)}, u32[]{:S(2)}, u32[]{:S(2)}) collective-permute-start(bf16[192,768]{1,0:T(8,128)(2,1)S(1)} %get-tuple-element.67), channel_id=1, source_target_pairs={{0,2},{1,3},{2,0},{3,1},{4,6},{5,7},{6,4},{7,5},{8,10},{9,11},{10,... | collective-permute-start | bytes 884744 | tf_op jit(solution)/shard_map/ppermute | solution.py:360
  121.4 7.6 %collective-permute-start.19 = (bf16[384,768]{1,0:T(8,128)(2,1)S(1)}, bf16[384,768]{1,0:T(8,128)(2,1)S(1)}, u32[]{:S(2)}, u32[]{:S(2)}) collective-permute-start(bf16[384,768]{1,0:T(8,128)(2,1)S(1)} %pad_maximum_fusion.11), channel_id=1, source_target_pairs={{0,1},{1,0},{2,3},{3,2},{4,5},{5,4},{6,7},{7,6},{8,9},{9,8},{10,11... | collective-permute-start | bytes 1769480 | tf_op jit(solution)/shard_map/ppermute | solution.py:360
  127.9 5.9 %collective-permute-start.15 = (bf16[384,768]{1,0:T(8,128)(2,1)S(1)}, bf16[384,768]{1,0:T(8,128)(2,1)S(1)}, u32[]{:S(2)}, u32[]{:S(2)}) collective-permute-start(bf16[384,768]{1,0:T(8,128)(2,1)S(1)} %pad_maximum_fusion.10), channel_id=1, source_target_pairs={{0,1},{1,0},{2,3},{3,2},{4,5},{5,4},{6,7},{7,6},{8,9},{9,8},{10,11... | collective-permute-start | bytes 1769480 | tf_op jit(solution)/shard_map/ppermute | solution.py:360
  133.2 11.3 %collective-permute-start.20 = (bf16[384,768]{1,0:T(8,128)(2,1)S(1)}, bf16[384,768]{1,0:T(8,128)(2,1)S(1)}, u32[]{:S(2)}, u32[]{:S(2)}) collective-permute-start(bf16[384,768]{1,0:T(8,128)(2,1)S(1)} %get-tuple-element.78), channel_id=1, source_target_pairs={{0,1},{1,0},{2,3},{3,2},{4,5},{5,4},{6,7},{7,6},{8,9},{9,8},{10,11... | collective-permute-start | bytes 1769480 | tf_op jit(solution)/shard_map/ppermute | solution.py:360
  138.0 8.2 %collective-permute-start.16 = (bf16[384,768]{1,0:T(8,128)(2,1)S(1)}, bf16[384,768]{1,0:T(8,128)(2,1)S(1)}, u32[]{:S(2)}, u32[]{:S(2)}) collective-permute-start(bf16[384,768]{1,0:T(8,128)(2,1)S(1)} %get-tuple-element.71), channel_id=1, source_target_pairs={{0,1},{1,0},{2,3},{3,2},{4,5},{5,4},{6,7},{7,6},{8,9},{9,8},{10,11... | collective-permute-start | bytes 1769480 | tf_op jit(solution)/shard_map/ppermute | solution.py:360
  140.6 21.4 %collective-permute-start.43 = (bf16[384,768]{1,0:T(8,128)(2,1)S(1)}, bf16[384,768]{1,0:T(8,128)(2,1)S(1)}, u32[]{:S(2)}, u32[]{:S(2)}) collective-permute-start(bf16[384,768]{1,0:T(8,128)(2,1)S(1)} %constant_dynamic-slice_fusion), channel_id=1, source_target_pairs={{0,4},{4,0},{8,12},{12,8},{16,20},{20,16},{24,28},{28,24},{1,5},{5... | collective-permute-start | bytes 1769480 | tf_op jit(solution)/shard_map/ppermute | solution.py:360
  144.6 9.9 %collective-permute-start.21 = (bf16[192,768]{1,0:T(8,128)(2,1)S(1)}, bf16[192,768]{1,0:T(8,128)(2,1)S(1)}, u32[]{:S(2)}, u32[]{:S(2)}) collective-permute-start(bf16[192,768]{1,0:T(8,128)(2,1)S(1)} %add_convert_fusion.5), channel_id=1, source_target_pairs={{0,2},{1,3},{2,0},{3,1},{4,6},{5,7},{6,4},{7,5},{8,10},{9,11},{10,... | collective-permute-start | bytes 884744 | tf_op jit(solution)/shard_map/ppermute | solution.py:360
  146.3 13.9 %collective-permute-start.17 = (bf16[192,768]{1,0:T(8,128)(2,1)S(1)}, bf16[192,768]{1,0:T(8,128)(2,1)S(1)}, u32[]{:S(2)}, u32[]{:S(2)}) collective-permute-start(bf16[192,768]{1,0:T(8,128)(2,1)S(1)} %add_convert_fusion.6), channel_id=1, source_target_pairs={{0,2},{1,3},{2,0},{3,1},{4,6},{5,7},{6,4},{7,5},{8,10},{9,11},{10,... | collective-permute-start | bytes 884744 | tf_op jit(solution)/shard_map/ppermute | solution.py:360
  160.7 6.6 %collective-permute-start.51 = (f32[4,768]{1,0:T(4,128)S(1)}, f32[4,768]{1,0:T(4,128)S(1)}, u32[]{:S(2)}, u32[]{:S(2)}) collective-permute-start(f32[4,768]{1,0:T(4,128)S(1)} %pad_maximum_fusion.12), channel_id=1, source_target_pairs={{0,1},{1,0},{2,3},{3,2},{4,5},{5,4},{6,7},{7,6},{8,9},{9,8},{10,11... | collective-permute-start | bytes 36872 | tf_op jit(solution)/shard_map/ppermute | solution.py:360
  162.7 12.7 %collective-permute-start.46 = (bf16[96,768]{1,0:T(8,128)(2,1)S(1)}, bf16[96,768]{1,0:T(8,128)(2,1)S(1)}, u32[]{:S(2)}, u32[]{:S(2)}) collective-permute-start(bf16[96,768]{1,0:T(8,128)(2,1)S(1)} %get-tuple-element.99), channel_id=1, source_target_pairs={{0,24},{4,28},{8,0},{12,4},{16,8},{20,12},{24,16},{28,20},{1,25},{... | collective-permute-start | bytes 442376 | tf_op jit(solution)/shard_map/ppermute | solution.py:373
  166.1 13.4 %collective-permute-start.45 = (bf16[96,768]{1,0:T(8,128)(2,1)S(1)}, bf16[96,768]{1,0:T(8,128)(2,1)S(1)}, u32[]{:S(2)}, u32[]{:S(2)}) collective-permute-start(bf16[96,768]{1,0:T(8,128)(2,1)S(1)} %get-tuple-element.98), channel_id=1, source_target_pairs={{0,16},{4,20},{8,24},{12,28},{16,0},{20,4},{24,8},{28,12},{1,17},{... | collective-permute-start | bytes 442376 | tf_op jit(solution)/shard_map/ppermute | solution.py:373
  166.1 13.4 %collective-permute-start.44 = (bf16[96,768]{1,0:T(8,128)(2,1)S(1)}, bf16[96,768]{1,0:T(8,128)(2,1)S(1)}, u32[]{:S(2)}, u32[]{:S(2)}) collective-permute-start(bf16[96,768]{1,0:T(8,128)(2,1)S(1)} %get-tuple-element.97), channel_id=1, source_target_pairs={{0,8},{4,12},{8,16},{12,20},{16,24},{20,28},{24,0},{28,4},{1,9},{5... | collective-permute-start | bytes 442376 | tf_op jit(solution)/shard_map/ppermute | solution.py:373
  167.4 3.8 %collective-permute-start.52 = (f32[4,768]{1,0:T(4,128)S(1)}, f32[4,768]{1,0:T(4,128)S(1)}, u32[]{:S(2)}, u32[]{:S(2)}) collective-permute-start(f32[4,768]{1,0:T(4,128)S(1)} %fusion.31), channel_id=1, source_target_pairs={{0,2},{1,3},{2,0},{3,1},{4,6},{5,7},{6,4},{7,5},{8,10},{9,11},{10,... | collective-permute-start | bytes 36872 | tf_op jit(solution)/shard_map/ppermute | solution.py:360
  169.1 14.1 %collective-permute-start.23 = (bf16[192,768]{1,0:T(8,128)(2,1)S(1)}, bf16[192,768]{1,0:T(8,128)(2,1)S(1)}, u32[]{:S(2)}, u32[]{:S(2)}) collective-permute-start(bf16[192,768]{1,0:T(8,128)(2,1)S(1)} %get-tuple-element.81), channel_id=1, source_target_pairs={{0,1},{1,0},{2,3},{3,2},{4,5},{5,4},{6,7},{7,6},{8,9},{9,8},{10,11... | collective-permute-start | bytes 884744 | tf_op jit(solution)/shard_map/ppermute | solution.py:360
  171.1 3.7 %collective-permute-start.53 = (f32[4,768]{1,0:T(4,128)S(1)}, f32[4,768]{1,0:T(4,128)S(1)}, u32[]{:S(2)}, u32[]{:S(2)}) collective-permute-start(f32[4,768]{1,0:T(4,128)S(1)} %add.198), channel_id=1, source_target_pairs={{0,4},{4,0},{8,12},{12,8},{16,20},{20,16},{24,28},{28,24},{1,5},{5... | collective-permute-start | bytes 36872 | tf_op jit(solution)/shard_map/ppermute | solution.py:360
  174.8 33.6 %collective-permute-start.35 = (bf16[768,768]{1,0:T(8,128)(2,1)S(1)}, bf16[768,768]{1,0:T(8,128)(2,1)S(1)}, u32[]{:S(2)}, u32[]{:S(2)}) collective-permute-start(bf16[768,768]{1,0:T(8,128)(2,1)S(1)} %fusion.4), channel_id=1, source_target_pairs={{0,4},{4,0},{8,12},{12,8},{16,20},{20,16},{24,28},{28,24},{1,5},{5... | collective-permute-start | bytes 3538952 | tf_op jit(solution)/shard_map/ppermute | solution.py:360
  175.4 7.8 %collective-permute-start.22 = (bf16[192,768]{1,0:T(8,128)(2,1)S(1)}, bf16[192,768]{1,0:T(8,128)(2,1)S(1)}, u32[]{:S(2)}, u32[]{:S(2)}) collective-permute-start(bf16[192,768]{1,0:T(8,128)(2,1)S(1)} %get-tuple-element.80), channel_id=1, source_target_pairs={{0,1},{1,0},{2,3},{3,2},{4,5},{5,4},{6,7},{7,6},{8,9},{9,8},{10,11... | collective-permute-start | bytes 884744 | tf_op jit(solution)/shard_map/ppermute | solution.py:360
  179.5 3.7 %collective-permute-start.54 = (f32[4,768]{1,0:T(4,128)S(1)}, f32[4,768]{1,0:T(4,128)S(1)}, u32[]{:S(2)}, u32[]{:S(2)}) collective-permute-start(f32[4,768]{1,0:T(4,128)S(1)} %add.199), channel_id=1, source_target_pairs={{0,8},{4,12},{8,0},{12,4},{16,24},{20,28},{24,16},{28,20},{1,9},{5... | collective-permute-start | bytes 36872 | tf_op jit(solution)/shard_map/ppermute | solution.py:360
  179.6 63.5 %collective-permute-start.47 = (bf16[96,768]{1,0:T(8,128)(2,1)S(1)}, bf16[96,768]{1,0:T(8,128)(2,1)S(1)}, u32[]{:S(2)}, u32[]{:S(2)}) collective-permute-start(bf16[96,768]{1,0:T(8,128)(2,1)S(1)} %add_convert_fusion.9.refs_0_), channel_id=1, source_target_pairs={{0,8},{4,12},{8,16},{12,20},{16,24},{20,28},{24,0},{28,4},{1,9},{5... | collective-permute-start | bytes 442376 | tf_op jit(solution)/shard_map/ppermute | solution.py:373
  196.8 45.9 %collective-permute-start.26 = (bf16[768,768]{1,0:T(8,128)(2,1)S(1)}, bf16[768,768]{1,0:T(8,128)(2,1)S(1)}, u32[]{:S(2)}, u32[]{:S(2)}) collective-permute-start(bf16[768,768]{1,0:T(8,128)(2,1)S(1)} %pad_maximum_fusion.6), channel_id=1, source_target_pairs={{0,2},{1,3},{2,0},{3,1},{4,6},{5,7},{6,4},{7,5},{8,10},{9,11},{10,... | collective-permute-start | bytes 3538952 | tf_op jit(solution)/shard_map/ppermute | solution.py:360
  209.3 8.9 %collective-permute-start.38 = (bf16[192,768]{1,0:T(8,128)(2,1)S(1)}, bf16[192,768]{1,0:T(8,128)(2,1)S(1)}, u32[]{:S(2)}, u32[]{:S(2)}) collective-permute-start(bf16[192,768]{1,0:T(8,128)(2,1)S(1)} %get-tuple-element.93), channel_id=1, source_target_pairs={{0,24},{4,28},{8,0},{12,4},{16,8},{20,12},{24,16},{28,20},{1,25},{... | collective-permute-start | bytes 884744 | tf_op jit(solution)/shard_map/ppermute | solution.py:373
  210.7 30.2 %collective-permute-start.37 = (bf16[192,768]{1,0:T(8,128)(2,1)S(1)}, bf16[192,768]{1,0:T(8,128)(2,1)S(1)}, u32[]{:S(2)}, u32[]{:S(2)}) collective-permute-start(bf16[192,768]{1,0:T(8,128)(2,1)S(1)} %get-tuple-element.92), channel_id=1, source_target_pairs={{0,16},{4,20},{8,24},{12,28},{16,0},{20,4},{24,8},{28,12},{1,17},{... | collective-permute-start | bytes 884744 | tf_op jit(solution)/shard_map/ppermute | solution.py:373
  210.8 30.0 %collective-permute-start.36 = (bf16[192,768]{1,0:T(8,128)(2,1)S(1)}, bf16[192,768]{1,0:T(8,128)(2,1)S(1)}, u32[]{:S(2)}, u32[]{:S(2)}) collective-permute-start(bf16[192,768]{1,0:T(8,128)(2,1)S(1)} %get-tuple-element.91), channel_id=1, source_target_pairs={{0,8},{4,12},{8,16},{12,20},{16,24},{20,28},{24,0},{28,4},{1,9},{5... | collective-permute-start | bytes 884744 | tf_op jit(solution)/shard_map/ppermute | solution.py:373
  218.2 25.5 %collective-permute-start.48 = (bf16[96,768]{1,0:T(8,128)(2,1)S(1)}, bf16[96,768]{1,0:T(8,128)(2,1)S(1)}, u32[]{:S(2)}, u32[]{:S(2)}) collective-permute-start(bf16[96,768]{1,0:T(8,128)(2,1)S(1)} %add_convert_fusion.9.refs_0_), channel_id=1, source_target_pairs={{0,16},{4,20},{8,24},{12,28},{16,0},{20,4},{24,8},{28,12},{1,17},{... | collective-permute-start | bytes 442376 | tf_op jit(solution)/shard_map/ppermute | solution.py:373
  240.9 5.7 %collective-permute-start.49 = (bf16[96,768]{1,0:T(8,128)(2,1)S(1)}, bf16[96,768]{1,0:T(8,128)(2,1)S(1)}, u32[]{:S(2)}, u32[]{:S(2)}) collective-permute-start(bf16[96,768]{1,0:T(8,128)(2,1)S(1)} %add_convert_fusion.9.refs_0_), channel_id=1, source_target_pairs={{0,24},{4,28},{8,0},{12,4},{16,8},{20,12},{24,16},{28,20},{1,25},{... | collective-permute-start | bytes 442376 | tf_op jit(solution)/shard_map/ppermute | solution.py:373
  240.9 6.9 %collective-permute-start.55 = (f32[4,768]{1,0:T(4,128)S(1)}, f32[4,768]{1,0:T(4,128)S(1)}, u32[]{:S(2)}, u32[]{:S(2)}) collective-permute-start(f32[4,768]{1,0:T(4,128)S(1)} %add.200), channel_id=1, source_target_pairs={{0,16},{4,20},{8,24},{12,28},{16,0},{20,4},{24,8},{28,12},{1,17},{... | collective-permute-start | bytes 36872 | tf_op jit(solution)/shard_map/ppermute | solution.py:360
  242.7 36.2 %collective-permute-start.24 = (bf16[512,768]{1,0:T(8,128)(2,1)S(1)}, bf16[512,768]{1,0:T(8,128)(2,1)S(1)}, u32[]{:S(2)}, u32[]{:S(2)}) collective-permute-start(bf16[512,768]{1,0:T(8,128)(2,1)S(1)} %add_convert_fusion.3), channel_id=1, source_target_pairs={{0,1},{1,0},{2,3},{3,2},{4,5},{5,4},{6,7},{7,6},{8,9},{9,8},{10,11... | collective-permute-start | bytes 2359304 | tf_op jit(solution)/shard_map/ppermute | solution.py:360
  243.1 11.8 %collective-permute-start.39 = (bf16[192,768]{1,0:T(8,128)(2,1)S(1)}, bf16[192,768]{1,0:T(8,128)(2,1)S(1)}, u32[]{:S(2)}, u32[]{:S(2)}) collective-permute-start(bf16[192,768]{1,0:T(8,128)(2,1)S(1)} %add_convert_fusion.4.refs_0_), channel_id=1, source_target_pairs={{0,8},{4,12},{8,16},{12,20},{16,24},{20,28},{24,0},{28,4},{1,9},{5... | collective-permute-start | bytes 884744 | tf_op jit(solution)/shard_map/ppermute | solution.py:373
  243.7 23.4 %collective-permute-start.40 = (bf16[192,768]{1,0:T(8,128)(2,1)S(1)}, bf16[192,768]{1,0:T(8,128)(2,1)S(1)}, u32[]{:S(2)}, u32[]{:S(2)}) collective-permute-start(bf16[192,768]{1,0:T(8,128)(2,1)S(1)} %add_convert_fusion.4.refs_0_), channel_id=1, source_target_pairs={{0,16},{4,20},{8,24},{12,28},{16,0},{20,4},{24,8},{28,12},{1,17},{... | collective-permute-start | bytes 884744 | tf_op jit(solution)/shard_map/ppermute | solution.py:373
  246.5 20.5 %collective-permute-start.41 = (bf16[192,768]{1,0:T(8,128)(2,1)S(1)}, bf16[192,768]{1,0:T(8,128)(2,1)S(1)}, u32[]{:S(2)}, u32[]{:S(2)}) collective-permute-start(bf16[192,768]{1,0:T(8,128)(2,1)S(1)} %add_convert_fusion.4.refs_0_), channel_id=1, source_target_pairs={{0,24},{4,28},{8,0},{12,4},{16,8},{20,12},{24,16},{28,20},{1,25},{... | collective-permute-start | bytes 884744 | tf_op jit(solution)/shard_map/ppermute | solution.py:373
  247.8 22.4 %collective-permute-start.27 = (bf16[384,768]{1,0:T(8,128)(2,1)S(1)}, bf16[384,768]{1,0:T(8,128)(2,1)S(1)}, u32[]{:S(2)}, u32[]{:S(2)}) collective-permute-start(bf16[384,768]{1,0:T(8,128)(2,1)S(1)} %constant_dynamic-slice_fusion.1), channel_id=1, source_target_pairs={{0,4},{4,0},{8,12},{12,8},{16,20},{20,16},{24,28},{28,24},{1,5},{5... | collective-permute-start | bytes 1769480 | tf_op jit(solution)/shard_map/ppermute | solution.py:360
  254.9 37.8 %collective-permute-start.50 = (bf16[384,768]{1,0:T(8,128)(2,1)S(1)}, bf16[384,768]{1,0:T(8,128)(2,1)S(1)}, u32[]{:S(2)}, u32[]{:S(2)}) collective-permute-start(bf16[384,768]{1,0:T(8,128)(2,1)S(1)} %spread_shards.5.own_ref), channel_id=1, source_target_pairs={{0,4},{4,0},{8,12},{12,8},{16,20},{20,16},{24,28},{28,24},{1,5},{5... | collective-permute-start | bytes 1769480 | tf_op jit(solution)/shard_map/ppermute | solution.py:360
  267.7 32.7 %collective-permute-start.42 = (bf16[768,768]{1,0:T(8,128)(2,1)S(1)}, bf16[768,768]{1,0:T(8,128)(2,1)S(1)}, u32[]{:S(2)}, u32[]{:S(2)}) collective-permute-start(bf16[768,768]{1,0:T(8,128)(2,1)S(1)} %spread_shards.4.own_ref), channel_id=1, source_target_pairs={{0,4},{4,0},{8,12},{12,8},{16,20},{20,16},{24,28},{28,24},{1,5},{5... | collective-permute-start | bytes 3538952 | tf_op jit(solution)/shard_map/ppermute | solution.py:360
  270.9 11.1 %collective-permute-start.30 = (bf16[96,768]{1,0:T(8,128)(2,1)S(1)}, bf16[96,768]{1,0:T(8,128)(2,1)S(1)}, u32[]{:S(2)}, u32[]{:S(2)}) collective-permute-start(bf16[96,768]{1,0:T(8,128)(2,1)S(1)} %get-tuple-element.85), channel_id=1, source_target_pairs={{0,24},{4,28},{8,0},{12,4},{16,8},{20,12},{24,16},{28,20},{1,25},{... | collective-permute-start | bytes 442376 | tf_op jit(solution)/shard_map/ppermute | solution.py:373
  277.7 13.8 %collective-permute-start.29 = (bf16[96,768]{1,0:T(8,128)(2,1)S(1)}, bf16[96,768]{1,0:T(8,128)(2,1)S(1)}, u32[]{:S(2)}, u32[]{:S(2)}) collective-permute-start(bf16[96,768]{1,0:T(8,128)(2,1)S(1)} %get-tuple-element.84), channel_id=1, source_target_pairs={{0,16},{4,20},{8,24},{12,28},{16,0},{20,4},{24,8},{28,12},{1,17},{... | collective-permute-start | bytes 442376 | tf_op jit(solution)/shard_map/ppermute | solution.py:373
  278.9 12.6 %collective-permute-start.28 = (bf16[96,768]{1,0:T(8,128)(2,1)S(1)}, bf16[96,768]{1,0:T(8,128)(2,1)S(1)}, u32[]{:S(2)}, u32[]{:S(2)}) collective-permute-start(bf16[96,768]{1,0:T(8,128)(2,1)S(1)} %get-tuple-element.83), channel_id=1, source_target_pairs={{0,8},{4,12},{8,16},{12,20},{16,24},{20,28},{24,0},{28,4},{1,9},{5... | collective-permute-start | bytes 442376 | tf_op jit(solution)/shard_map/ppermute | solution.py:373
  282.0 16.5 %collective-permute-start.25 = (bf16[128,768]{1,0:T(8,128)(2,1)S(1)}, bf16[128,768]{1,0:T(8,128)(2,1)S(1)}, u32[]{:S(2)}, u32[]{:S(2)}) collective-permute-start(bf16[128,768]{1,0:T(8,128)(2,1)S(1)} %dynamic-slice_convert_fusion), channel_id=1, source_target_pairs={{1,2},{2,1},{3,4},{4,3},{5,6},{6,5},{7,8},{8,7},{9,10},{10,9},{11,... | collective-permute-start | bytes 589832 | tf_op jit(solution)/shard_map/ppermute | solution.py:368
  291.6 9.6 %collective-permute-start.31 = (bf16[96,768]{1,0:T(8,128)(2,1)S(1)}, bf16[96,768]{1,0:T(8,128)(2,1)S(1)}, u32[]{:S(2)}, u32[]{:S(2)}) collective-permute-start(bf16[96,768]{1,0:T(8,128)(2,1)S(1)} %add_convert_fusion.10.refs_0_), channel_id=1, source_target_pairs={{0,8},{4,12},{8,16},{12,20},{16,24},{20,28},{24,0},{28,4},{1,9},{5... | collective-permute-start | bytes 442376 | tf_op jit(solution)/shard_map/ppermute | solution.py:373
  292.3 12.2 %collective-permute-start.32 = (bf16[96,768]{1,0:T(8,128)(2,1)S(1)}, bf16[96,768]{1,0:T(8,128)(2,1)S(1)}, u32[]{:S(2)}, u32[]{:S(2)}) collective-permute-start(bf16[96,768]{1,0:T(8,128)(2,1)S(1)} %add_convert_fusion.10.refs_0_), channel_id=1, source_target_pairs={{0,16},{4,20},{8,24},{12,28},{16,0},{20,4},{24,8},{28,12},{1,17},{... | collective-permute-start | bytes 442376 | tf_op jit(solution)/shard_map/ppermute | solution.py:373
  292.7 12.6 %collective-permute-start.33 = (bf16[96,768]{1,0:T(8,128)(2,1)S(1)}, bf16[96,768]{1,0:T(8,128)(2,1)S(1)}, u32[]{:S(2)}, u32[]{:S(2)}) collective-permute-start(bf16[96,768]{1,0:T(8,128)(2,1)S(1)} %add_convert_fusion.10.refs_0_), channel_id=1, source_target_pairs={{0,24},{4,28},{8,0},{12,4},{16,8},{20,12},{24,16},{28,20},{1,25},{... | collective-permute-start | bytes 442376 | tf_op jit(solution)/shard_map/ppermute | solution.py:373
  305.9 14.5 %collective-permute-start.34 = (bf16[384,768]{1,0:T(8,128)(2,1)S(1)}, bf16[384,768]{1,0:T(8,128)(2,1)S(1)}, u32[]{:S(2)}, u32[]{:S(2)}) collective-permute-start(bf16[384,768]{1,0:T(8,128)(2,1)S(1)} %spread_shards.3.own_ref), channel_id=1, source_target_pairs={{0,4},{4,0},{8,12},{12,8},{16,20},{20,16},{24,28},{28,24},{1,5},{5... | collective-permute-start | bytes 1769480 | tf_op jit(solution)/shard_map/ppermute | solution.py:360
  (70 other events, 298.1 us)
